TPU v7x, 256 devices: a whole 4x4x8 slice. The times are simulated.
256 devices in a mesh: dp: 4 (over x), expert: 64 (over z, y, core).
Axes of the slice: x: 4, y: 4, z: 8, core: 2. Of those that a mesh axis runs over, the one named last changes fastest.
Arguments:
- grad_parts: bfloat16 [4, 256, 192, 2048], P('dp', 'expert'), may hold values from -4 to 4
- old_m_codes: bfloat16 [4, 64, 576, 2048], P('dp', 'expert'), may hold values from -1 to 1
- old_v_codes: bfloat16 [4, 64, 576, 2048], P('dp', 'expert'), may hold values from 0.049804688 to 1
- old_m_scale: bfloat16 [4, 64, 576, 16], P('dp', 'expert'), may hold values from 0.049804688 to 1
- old_v_scale: bfloat16 [4, 64, 576, 16], P('dp', 'expert'), may hold values from 0.049804688 to 1
- expert_map: int32 [256], replicated, may hold values from 0 to 255, as said below
- slot_expert: int32 [64, 576], P('expert'), may hold values from 0 to 255, as said below
- slot_row: int32 [64, 576], P('expert'), may hold values from 0 to 47
- peer_count: int32 [64, 64], P('expert'), may hold values from 0 to 9, as said below
- peer_offset: int32 [64, 64], P('expert'), may hold values from 0 to 567, as said below
Outputs:
- direction: float32 [256, 192, 2048], P('expert', 'dp')
- new_codes: bfloat16 [2, 256, 192, 2048], P(None, 'expert', 'dp')
- new_scales: bfloat16 [2, 256, 192, 16], P(None, 'expert', 'dp')
Inputs may be any that keep to these rules, and one draw needn't show every extreme that they name: expert_map is a permutation. `slot_expert`: each row of the new layout, on each dp index, is held by exactly one live slot; slots past a reader's load hold 0. `peer_count`: A reader's slots are ordered by owner; each owner receives 192 rows in all; some reader holds 9 slots for every owner, and 4 readers hold none. peer_offset is the running total of peer_count over owners before each.
All inputs are finite; a program needn't handle non-finite values. Where the computation divides by a largest or mean magnitude, that divisor is 1e-20 or more.
Results may differ from a plain program's by a relative error of at most 0.018.
Values may be sent and summed in bfloat16 or wider, within the bound.
A program may use at most 128 MiB of HBM per device.

v0:
```python
import jax
import jax.numpy as jnp
from jax import lax
from jax.sharding import PartitionSpec as P

beta_one = 0.9
beta_two = 0.95
adam_eps = 1e-08
scale_eps = 1e-06


def dequantize(code_array, block_scale):
    full_shape = code_array.shape
    blocks = code_array.astype(jnp.float32).reshape(
        full_shape[:-1] + (block_scale.shape[-1], full_shape[-1] // block_scale.shape[-1])
    )
    return (blocks * block_scale.astype(jnp.float32)[..., None]).reshape(full_shape)


def quantize(values, block_count):
    full_shape = values.shape
    blocks = values.reshape(full_shape[:-1] + (block_count, full_shape[-1] // block_count))
    block_scale = (jnp.max(jnp.abs(blocks), axis=-1) + scale_eps).astype(jnp.bfloat16)
    code_array = (blocks / block_scale.astype(jnp.float32)[..., None]).astype(jnp.bfloat16)
    return (code_array.reshape(full_shape), block_scale)


def per_device(
    grad_parts,
    old_m_codes,
    old_v_codes,
    old_m_scale,
    old_v_scale,
    expert_map,
    slot_expert,
    slot_row,
    peer_count,
    peer_offset,
):
    owners = lax.axis_size("expert")
    codes_first = old_m_codes[0, 0]
    codes_second = old_v_codes[0, 0]
    scale_first = old_m_scale[0, 0]
    scale_second = old_v_scale[0, 0]
    slot_total = codes_first.shape[0]
    width = codes_first.shape[1]
    block_count = scale_first.shape[1]
    per_peer = slot_total // owners
    exp_dev = grad_parts.shape[1]
    share_rows = grad_parts.shape[2] // lax.axis_size("dp")
    owned_rows = exp_dev * share_rows
    send_counts = peer_count[0]
    offsets = peer_offset[0]
    slot_place = jnp.arange(per_peer, dtype=jnp.int32)[None, :]
    picked = (offsets[:, None] + slot_place).reshape(-1)
    new_expert = expert_map[slot_expert[0]]
    local_all = new_expert % exp_dev * share_rows + slot_row[0]
    usable = slot_place < send_counts[:, None]
    targets = jnp.where(usable, local_all[picked].reshape(owners, per_peer), -1)
    arrived_targets = lax.all_to_all(targets, "expert", split_axis=0, concat_axis=0, tiled=True)
    sent_first = dequantize(codes_first[picked], scale_first[picked]).reshape(
        owners, per_peer, width
    )
    sent_second = dequantize(codes_second[picked], scale_second[picked]).reshape(
        owners, per_peer, width
    )
    first_rows = lax.all_to_all(
        sent_first.astype(jnp.bfloat16), "expert", split_axis=0, concat_axis=0, tiled=True
    ).astype(sent_first.dtype)
    second_rows = lax.all_to_all(
        sent_second.astype(jnp.bfloat16), "expert", split_axis=0, concat_axis=0, tiled=True
    ).astype(sent_second.dtype)
    flat_targets = arrived_targets.reshape(-1)
    landing = jnp.where(flat_targets >= 0, flat_targets, owned_rows)
    first_moment = (
        jnp.zeros((owned_rows, width), jnp.float32)
        .at[landing]
        .set(first_rows.reshape(-1, width), mode="drop")
    )
    second_moment = (
        jnp.zeros((owned_rows, width), jnp.float32)
        .at[landing]
        .set(second_rows.reshape(-1, width), mode="drop")
    )
    first_moment, second_moment = (
        first_moment.reshape(exp_dev, share_rows, width),
        second_moment.reshape(exp_dev, share_rows, width),
    )
    grad_share = lax.psum_scatter(grad_parts[0], "dp", scatter_dimension=1, tiled=True).astype(
        jnp.float32
    )
    first_new = beta_one * first_moment + (1.0 - beta_one) * grad_share
    second_new = beta_two * second_moment + (1.0 - beta_two) * grad_share * grad_share
    direction = first_new / (jnp.sqrt(second_new) + adam_eps)
    code_first, new_scale_first = quantize(first_new, block_count)
    code_second, new_scale_second = quantize(second_new, block_count)
    return (
        direction,
        jnp.stack([code_first, code_second]),
        jnp.stack([new_scale_first, new_scale_second]),
    )


def solution(mesh):
    in_specs = (
        P("dp", "expert", None, None),
        P("dp", "expert", None, None),
        P("dp", "expert", None, None),
        P("dp", "expert", None, None),
        P("dp", "expert", None, None),
        P(),
        P("expert", None),
        P("expert", None),
        P("expert", None),
        P("expert", None),
    )
    out_specs = (
        P("expert", "dp", None),
        P(None, "expert", "dp", None),
        P(None, "expert", "dp", None),
    )
    return jax.shard_map(
        per_device, mesh=mesh, in_specs=in_specs, out_specs=out_specs, check_vma=False
    )
```

profile of v0, /device:TPU:1, one launch (start us, length us, event | category | flops | bytes accessed | tf_op | source)
XLA Modules:
  0.0 314.9 jit_solution(14534347381764217712)
XLA Ops:
  9.0 3.9 %gather_fusion = s32[576]{0:T(1024)S(1)} fusion(s32[256]{0:T(256)S(1)} %copy-done.2, s32[1024]{0:T(1024)S(1)} %pad_clamp_fusion.1), kind=kCustom, calls=%fused_computation | custom fusion | bytes 6912 | tf_op jit(solution)/shard_map/gather | solution.py:56
  13.0 2.6 gather_fusion.1
  16.4 13.2 %all-to-all-start = ((s32[64,1,9]{2,1,0:T(1,128)}), s32[64,1,9]{2,1,0:T(1,128)S(1)}, u32[]{:S(2)}, u32[]{:S(2)}) async-start(s32[64,1,9]{2,1,0:T(1,128)} %bitcast.3), calls=%async_computation | async-start | bytes 65536 | tf_op jit(solution)/shard_map/all_to_all | solution.py:60
  31.7 3.4 %mul.71 = f32[576,16,128]{2,1,0:T(8,128)} broadcast(bf16[576,16]{1,0:T(8,128)(2,1)S(1)} %gather_fusion.5), dimensions={0,1} | broadcast | bytes 4737024 | tf_op jit(solution)/shard_map/mul | solution.py:17
  35.1 6.8 %mul.72 = f32[64,9,2048]{2,1,0:T(8,128)} reshape(f32[576,16,128]{2,1,0:T(8,128)} %mul.71) | data formatting | bytes 9437184 | tf_op jit(solution)/shard_map/mul | solution.py:17
  41.9 4.0 %gather_fusion.4 = bf16[576,2048]{1,0:T(8,128)(2,1)} fusion(bf16[576,2048]{1,0:T(8,128)(2,1)S(1)} %bitcast.36, s32[1024]{0:T(1024)S(1)} %pad_clamp_fusion), kind=kCustom, calls=%fused_computation.4 | custom fusion | bytes 4720896 | tf_op jit(solution)/shard_map/gather | solution.py:64
  45.9 5.7 %reshape.249 = f32[64,9,2048]{2,1,0:T(8,128)} reshape(bf16[576,2048]{1,0:T(8,128)(2,1)} %gather_fusion.4) | data formatting | bytes 7077888 | tf_op jit(solution)/shard_map/convert_element_type | solution.py:14
  51.5 9.2 %multiply_convert_fusion = bf16[64,9,2048]{2,1,0:T(8,128)(2,1)} fusion(f32[64,9,2048]{2,1,0:T(8,128)} %reshape.249, f32[64,9,2048]{2,1,0:T(8,128)} %mul.72), kind=kLoop, calls=%fused_computation.8 | loop fusion | flops 2359296 | bytes 11796480 | tf_op jit(solution)/shard_map/convert_element_type | solution.py:71
  60.7 10.5 %all-to-all-start.2 = ((bf16[64,9,2048]{2,1,0:T(8,128)(2,1)}), bf16[64,9,2048]{2,1,0:T(8,128)(2,1)}, u32[]{:S(2)}, u32[]{:S(2)}) async-start(bf16[64,9,2048]{2,1,0:T(8,128)(2,1)} %multiply_convert_fusion), calls=%async_computation.3 | async-start | bytes 8388608 | tf_op jit(solution)/shard_map/all_to_all | solution.py:70
  74.1 3.4 %mul.63 = f32[576,16,128]{2,1,0:T(8,128)} broadcast(bf16[576,16]{1,0:T(8,128)(2,1)S(1)} %gather_fusion.3), dimensions={0,1} | broadcast | bytes 4737024 | tf_op jit(solution)/shard_map/mul | solution.py:17
  77.5 6.9 %mul.64 = f32[64,9,2048]{2,1,0:T(8,128)} reshape(f32[576,16,128]{2,1,0:T(8,128)} %mul.63) | data formatting | bytes 9437184 | tf_op jit(solution)/shard_map/mul | solution.py:17
  84.4 4.1 %gather_fusion.2 = bf16[576,2048]{1,0:T(8,128)(2,1)} fusion(bf16[576,2048]{1,0:T(8,128)(2,1)S(1)} %bitcast.37, s32[1024]{0:T(1024)S(1)} %pad_clamp_fusion), kind=kCustom, calls=%fused_computation.2 | custom fusion | bytes 4720896 | tf_op jit(solution)/shard_map/gather | solution.py:61
  88.5 5.7 %reshape.246 = f32[64,9,2048]{2,1,0:T(8,128)} reshape(bf16[576,2048]{1,0:T(8,128)(2,1)} %gather_fusion.2) | data formatting | bytes 7077888 | tf_op jit(solution)/shard_map/convert_element_type | solution.py:14
  94.2 9.4 %multiply_convert_fusion.1 = bf16[64,9,2048]{2,1,0:T(8,128)(2,1)} fusion(f32[64,9,2048]{2,1,0:T(8,128)} %reshape.246, f32[64,9,2048]{2,1,0:T(8,128)} %mul.64), kind=kLoop, calls=%fused_computation.9 | loop fusion | flops 2359296 | bytes 11796480 | tf_op jit(solution)/shard_map/convert_element_type | solution.py:68
  103.5 62.1 %all-to-all-done.2 = bf16[64,9,2048]{2,1,0:T(8,128)(2,1)} async-done(((bf16[64,9,2048]{2,1,0:T(8,128)(2,1)}), bf16[64,9,2048]{2,1,0:T(8,128)(2,1)}, u32[]{:S(2)}, u32[]{:S(2)}) %all-to-all-start.2) | async-done | bytes 2359328 | tf_op jit(solution)/shard_map/all_to_all | solution.py:70
  165.6 7.4 %all-to-all-start.1 = ((bf16[64,9,2048]{2,1,0:T(8,128)(2,1)}), bf16[64,9,2048]{2,1,0:T(8,128)(2,1)}, u32[]{:S(2)}, u32[]{:S(2)}) async-start(bf16[64,9,2048]{2,1,0:T(8,128)(2,1)} %multiply_convert_fusion.1), calls=%async_computation.1 | async-start | bytes 8388608 | tf_op jit(solution)/shard_map/all_to_all | solution.py:67
  174.4 5.1 %reshape.312 = f32[576,2048]{1,0:T(8,128)} reshape(bf16[64,9,2048]{2,1,0:T(8,128)(2,1)} %all-to-all-done.2) | data formatting | bytes 7077888 | tf_op jit(solution)/shard_map/reshape | solution.py:83
  179.6 10.4 %scatter_custom_fusion.1 = f32[192,2048]{1,0:T(8,128)} fusion(s32[576]{0:T(1024)S(1)} %fusion.20, f32[576,2048]{1,0:T(8,128)} %reshape.312, f32[]{:T(128)} %constant.16.clone.1), kind=kCustom, calls=%fused_computation.22 | custom fusion | bytes 1573376 | tf_op jit(solution)/shard_map/scatter | solution.py:83
  189.9 77.7 %all-to-all-done.1 = bf16[64,9,2048]{2,1,0:T(8,128)(2,1)} async-done(((bf16[64,9,2048]{2,1,0:T(8,128)(2,1)}), bf16[64,9,2048]{2,1,0:T(8,128)(2,1)}, u32[]{:S(2)}, u32[]{:S(2)}) %all-to-all-start.1) | async-done | bytes 2359328 | tf_op jit(solution)/shard_map/all_to_all | solution.py:67
  267.7 5.1 %reshape.304 = f32[576,2048]{1,0:T(8,128)} reshape(bf16[64,9,2048]{2,1,0:T(8,128)(2,1)} %all-to-all-done.1) | data formatting | bytes 7077888 | tf_op jit(solution)/shard_map/reshape | solution.py:78
  272.8 10.4 %scatter_custom_fusion = f32[192,2048]{1,0:T(8,128)} fusion(s32[576]{0:T(1024)S(1)} %fusion.20, f32[576,2048]{1,0:T(8,128)} %reshape.304, f32[]{:T(128)} %constant.16.clone.1), kind=kCustom, calls=%fused_computation.24 | custom fusion | bytes 1573376 | tf_op jit(solution)/shard_map/scatter | solution.py:78
  286.4 3.3 %fusion.8 = (f32[4,48,2048]{2,1,0:T(8,128)S(1)}, f32[4,48,2048]{2,1,0:T(8,128)}) fusion(f32[4,48,2048]{2,1,0:T(8,128)} %bitcast.40, bf16[4,48,2048]{2,1,0:T(8,128)(2,1)} %reduce-scatter.2.cloned.1.call-done, f32[4,48,2048]{2,1,0:T(8,128)S(1)} %bitcast.38), kind=kLoop, calls=%fused_computation.28 | loop fusion | flops 3145728 | bytes 7077888 | tf_op jit(solution)/shard_map/abs | solution.py:23
  298.4 2.6 div.32
  301.2 4.6 %fusion.6 = (bf16[1,4,48,2048]{3,2,1,0:T(8,128)(2,1)S(1)}, f32[4,48,2048]{2,1,0:T(8,128)}, bf16[1,4,48,2048]{3,2,1,0:T(8,128)(2,1)S(1)}) fusion(f32[4,48,2048]{2,1,0:T(8,128)} %div.29, f32[4,48,2048]{2,1,0:T(8,128)} %bitcast.41, bf16[4,48,2048]{2,1,0:T(8,128)(2,1)S(1)} %copy-done.5, f32[4,48,2048]{2,1,0:T(8,128)S(1)} %bitcast.39, f32[4,48,2048]{2,1,0:T(8,128)} %div.32), kind=kLoop, calls=%fused_computation.26 | loop fusion | flops 4718592 | bytes 10223616 | tf_op jit(solution)/shard_map/convert_element_type | solution.py:24
  (57 shorter events, 23.2 us)
Async XLA Ops:
  7.2 34.7 %copy-start = (bf16[1,1,576,2048]{3,2,1,0:T(8,128)(2,1)S(1)}, bf16[1,1,576,2048]{3,2,1,0:T(8,128)(2,1)}, u32[]{:S(2)}) copy-start(bf16[1,1,576,2048]{3,2,1,0:T(8,128)(2,1)} %param.12) | copy-start | bytes 7077892
  7.2 1.8 copy-start.2
  9.0 4.0 %copy-start.8 = (s32[1,576]{1,0:T(1,128)S(1)}, s32[1,576]{1,0:T(1,128)}, u32[]{:S(2)}) copy-start(s32[1,576]{1,0:T(1,128)} %param.17) | copy-start | bytes 6916
  13.0 2.8 copy-start.9
  13.0 16.6 %copy-start.6 = (bf16[1,1,576,16]{2,3,1,0:T(8,128)(2,1)S(1)}, bf16[1,1,576,16]{2,3,1,0:T(8,128)(2,1)}, u32[]{:S(2)}) copy-start(bf16[1,1,576,16]{2,3,1,0:T(8,128)(2,1)} %param.14) | copy-start | bytes 55300
  16.4 44.3 %all-to-all-start = ((s32[64,1,9]{2,1,0:T(1,128)}), s32[64,1,9]{2,1,0:T(1,128)S(1)}, u32[]{:S(2)}, u32[]{:S(2)}) async-start(s32[64,1,9]{2,1,0:T(1,128)} %bitcast.3), calls=%async_computation | async-start | bytes 65536 | tf_op jit(solution)/shard_map/all_to_all | solution.py:60
  60.7 104.9 %all-to-all-start.2 = ((bf16[64,9,2048]{2,1,0:T(8,128)(2,1)}), bf16[64,9,2048]{2,1,0:T(8,128)(2,1)}, u32[]{:S(2)}, u32[]{:S(2)}) async-start(bf16[64,9,2048]{2,1,0:T(8,128)(2,1)} %multiply_convert_fusion), calls=%async_computation.3 | async-start | bytes 8388608 | tf_op jit(solution)/shard_map/all_to_all | solution.py:70
  71.2 215.1 %reduce-scatter.2.cloned.1.call-start = ((), (), s32[]{:S(2)}) async-start(), calls=%async_computation.4 | async-start | bytes 3932160 | tf_op jit(solution)/shard_map/reduce_scatter | solution.py:89
  71.3 0.7 copy-start.7
  77.5 6.9 %copy-start.3 = (bf16[1,1,576,2048]{3,2,1,0:T(8,128)(2,1)S(1)}, bf16[1,1,576,2048]{3,2,1,0:T(8,128)(2,1)}, u32[]{:S(2)}) copy-start(bf16[1,1,576,2048]{3,2,1,0:T(8,128)(2,1)} %param.11) | copy-start | bytes 7077892
  165.6 102.1 %all-to-all-start.1 = ((bf16[64,9,2048]{2,1,0:T(8,128)(2,1)}), bf16[64,9,2048]{2,1,0:T(8,128)(2,1)}, u32[]{:S(2)}, u32[]{:S(2)}) async-start(bf16[64,9,2048]{2,1,0:T(8,128)(2,1)} %multiply_convert_fusion.1), calls=%async_computation.1 | async-start | bytes 8388608 | tf_op jit(solution)/shard_map/all_to_all | solution.py:67
  283.2 1.9 copy-start.4
  298.4 2.8 copy-start.5
  305.8 2.2 copy-start.1
Sparse Core Ops, SparseCore 0:
  74.6 41.7 reduce-scatter.1
where the time goes:
time: 317 us; the launch traced here: 315 us
  waiting for transfers between devices  141 us (44%)
  local copies, waits for them, and re-layouts  93.6 us (30%)
  other arithmetic  35.4 us (11%)
  starting transfers between devices  31.1 us (10%)
  between operations  14.3 us (5%)
    all_to_all x1, waiting for transfers between devices, per_device(): lax.all_to_all(sent_first.astype(jnp.bfloat16), 'expert', split_axis=0, c...  77.7 us
    all_to_all x1, waiting for transfers between devices, per_device(): lax.all_to_all(sent_second.astype(jnp.bfloat16), 'expert', split_axis=0,...  62.1 us
    mul x4, local copies, waits for them, and re-layouts, dequantize(): blocks * block_scale.astype(jnp.float32)[..., None]  20.4 us
    all_to_all x1, starting transfers between devices, per_device(): lax.all_to_all(targets, 'expert', split_axis=0, concat_axis=0, tiled=True)  13.2 us
    convert_element_type x2, local copies, waits for them, and re-layouts, dequantize(): code_array.astype(jnp.float32)  11.4 us
    all_to_all x1, starting transfers between devices, per_device(): lax.all_to_all(sent_second.astype(jnp.bfloat16), 'expert', split_axis=0,...  10.5 us
    scatter x1, local copies, waits for them, and re-layouts, per_device(): first_moment = jnp.zeros((owned_rows, width), jnp.float32).at[landing].se...  10.4 us
    scatter x1, local copies, waits for them, and re-layouts, per_device(): second_moment = jnp.zeros((owned_rows, width), jnp.float32).at[landing].s...  10.4 us
  transfers between devices with their start and end apart: 4, of which 2 were waited for; matrix products, arithmetic and copies ran while one was open for 31% of the time, Pallas kernels for 0%

commit v1 on v0

--- a/solution.py
+++ b/solution.py
@@ -1,12 +1,22 @@
+import functools
+
 import jax
 import jax.numpy as jnp
 from jax import lax
+from jax.experimental import pallas as pl
+from jax.experimental.pallas import tpu as pltpu
 from jax.sharding import PartitionSpec as P
 
 beta_one = 0.9
 beta_two = 0.95
 adam_eps = 1e-08
 scale_eps = 1e-06
+
+MESH = pl.DeviceIdType.MESH
+f32 = jnp.float32
+bf16 = jnp.bfloat16
+BASE = 4
+EXTRA = 5
 
 
 def dequantize(code_array, block_scale):
@@ -25,7 +35,7 @@
     return (code_array.reshape(full_shape), block_scale)
 
 
-def per_device(
+def padded_exchange(
     grad_parts,
     old_m_codes,
     old_v_codes,
@@ -101,6 +111,427 @@
     )
 
 
+def iota(shape, dim):
+    return lax.broadcasted_iota(jnp.int32, shape, dim)
+
+
+def dot(a, b, dims=((1,), (0,))):
+    return lax.dot_general(a, b, (dims, ((), ())), preferred_element_type=f32)
+
+
+def pick(rows, chosen, vector):
+    return jnp.sum(jnp.where(chosen, vector, 0.0), axis=1, keepdims=True)
+
+
+def resume_kernel(
+    grad_ref,
+    m_ref,
+    v_ref,
+    ms_ref,
+    vs_ref,
+    map_ref,
+    expert_ref,
+    row_ref,
+    count_ref,
+    offset_ref,
+    dir_ref,
+    codes_ref,
+    scales_ref,
+    flag_ref,
+    moments,
+    relay,
+    extra,
+    extra_core,
+    extra_y,
+    extra_z,
+    part_core,
+    part_y,
+    send,
+    recv,
+    meta_send,
+    meta_recv,
+    grads,
+    place,
+    late,
+    landed,
+    send_sem,
+    recv_sem,
+    meta_ssem,
+    meta_rsem,
+    grad_ssem,
+    grad_rsem,
+    core_sem,
+    y_ssem,
+    y_rsem,
+    z_ssem,
+    z_rsem,
+):
+    d = lax.axis_index("dp")
+    e = lax.axis_index("expert")
+    z, y, k = lax.div(e, 8), lax.rem(lax.div(e, 2), 4), lax.rem(e, 2)
+    share = grads.shape[2]
+
+    def peer(i):
+        pz = lax.rem(z + lax.div(i, 8), 8)
+        py = lax.rem(y + lax.rem(lax.div(i, 2), 4), 4)
+        pk = lax.rem(k + lax.rem(i, 2), 2)
+        return pz * 8 + py * 2 + pk
+
+    barrier = pltpu.get_barrier_semaphore()
+
+    def greet(i, carry):
+        pl.semaphore_signal(barrier, inc=1, device_id=(d, peer(i)), device_id_type=MESH)
+        return carry
+
+    lax.fori_loop(1, 64, greet, 0)
+    for dx in range(1, 4):
+        pl.semaphore_signal(
+            barrier, inc=1, device_id=(lax.rem(d + dx, 4), e), device_id_type=MESH
+        )
+
+    for b in range(16):
+        lanes = slice(b * 128, (b + 1) * 128)
+        moments[:, b * 128 : (b + 1) * 128] = (
+            m_ref[:, lanes].astype(f32) * ms_ref[:, b : b + 1].astype(f32)
+        ).astype(bf16)
+        moments[:, 2048 + b * 128 : 2048 + (b + 1) * 128] = (
+            v_ref[:, lanes].astype(f32) * vs_ref[:, b : b + 1].astype(f32)
+        ).astype(bf16)
+
+    count = count_ref[...].astype(f32)
+    offset = offset_ref[...].astype(f32)
+    slots = m_ref.shape[0]
+
+    row, col = iota((64 * EXTRA, 64), 0), iota((64 * EXTRA, 64), 1)
+    u = row & 63
+    owner = ((u & 7) << 3) | (((u >> 3) & 3) << 1) | (u >> 5)
+    chosen = owner == col
+    s = (iota((64 * EXTRA, 1), 0) >> 6).astype(f32) + float(BASE)
+    source = jnp.where(
+        s < pick(64 * EXTRA, chosen, count), pick(64 * EXTRA, chosen, offset) + s, -1.0
+    )
+    slot_lane = iota((64 * EXTRA, slots), 1).astype(f32)
+    take_extra = (slot_lane == source).astype(bf16)
+    for c in range(8):
+        rows = dot(take_extra, moments[:, c * 512 : (c + 1) * 512])
+        for s_i in range(EXTRA):
+            for q in range(4):
+                relay[pl.ds(s_i * 32 + c * 4 + q, 64, stride=32 * EXTRA), :] = rows[
+                    s_i * 64 : (s_i + 1) * 64, q * 128 : (q + 1) * 128
+                ]
+
+    def narrow(u, carry):
+        extra[u] = relay[pl.ds(pl.multiple_of(u * 32 * EXTRA, 32), 32 * EXTRA), :].astype(bf16)
+        return carry
+
+    lax.fori_loop(0, 64, narrow, 0)
+
+    orow, ocol = iota((64, 64), 0), iota((64, 64), 1)
+    count_col = pick(64, orow == ocol, count)
+    offset_col = pick(64, orow == ocol, offset)
+    lane = iota((64, slots), 1).astype(f32)
+    held = jnp.logical_and(lane >= offset_col, lane < offset_col + count_col)
+    rank = iota((1, slots), 1).astype(f32) - jnp.sum(
+        jnp.where(held, offset_col, 0.0), axis=0, keepdims=True
+    )
+    old = iota((256, slots), 0) == expert_ref[...]
+    mapped = dot(
+        jnp.broadcast_to(map_ref[...].astype(f32), (8, 256)).astype(bf16), old.astype(bf16)
+    )[0:1]
+    land = (mapped - 4.0 * jnp.floor(mapped * 0.25)) * float(share) + row_ref[...].astype(f32) + 1.0
+    held_land = jnp.where(held, land, 0.0).astype(bf16)
+    at_rank = (iota((128, slots), 0).astype(f32) == rank).astype(bf16)
+    targets = dot(held_land, at_rank, ((1,), (1,)))
+    shift = (iota((64, 128), 0) + 64 == iota((64, 128), 1)).astype(bf16)
+    counts = dot(jnp.broadcast_to(count, (64, 64)).astype(bf16), shift)
+    meta_send[...] = jnp.where(iota((64, 128), 1) < 16, targets, counts)
+
+    pl.semaphore_wait(barrier, 66)
+
+    def grad_copy(dx):
+        to = lax.rem(d + dx, 4)
+        return pltpu.make_async_remote_copy(
+            src_ref=grad_ref.at[0, :, pl.ds(pl.multiple_of(to * share, 16), share), :],
+            dst_ref=grads.at[dx],
+            send_sem=grad_ssem.at[dx],
+            recv_sem=grad_rsem.at[dx],
+            device_id=(to, e),
+            device_id_type=MESH,
+        )
+
+    own_grad = pltpu.make_async_copy(
+        grad_ref.at[0, :, pl.ds(pl.multiple_of(d * share, 16), share), :], grads.at[0], grad_ssem.at[0]
+    )
+    for dx in range(1, 4):
+        grad_copy(dx).start()
+    own_grad.start()
+
+    core_copy = pltpu.make_async_remote_copy(
+        src_ref=extra.at[pl.ds((1 - k) * 32, 32)],
+        dst_ref=extra_core,
+        send_sem=core_sem.at[0],
+        recv_sem=core_sem.at[1],
+        device_id=(d, peer(1)),
+        device_id_type=MESH,
+    )
+    core_copy.start()
+
+    def meta_copy(i):
+        to = peer(i)
+        return pltpu.make_async_remote_copy(
+            src_ref=meta_send.at[pl.ds(to, 1)],
+            dst_ref=meta_recv.at[pl.ds(i, 1)],
+            send_sem=meta_ssem.at[i],
+            recv_sem=meta_rsem.at[i],
+            device_id=(d, to),
+            device_id_type=MESH,
+        )
+
+    def main_copy(i):
+        to = peer(i)
+        return pltpu.make_async_remote_copy(
+            src_ref=send.at[to],
+            dst_ref=recv.at[i],
+            send_sem=send_sem.at[i],
+            recv_sem=recv_sem.at[i],
+            device_id=(d, to),
+            device_id_type=MESH,
+        )
+
+    def start_meta(i, carry):
+        meta_copy(i).start()
+        return carry
+
+    def start_main(i, carry):
+        main_copy(i).start()
+        return carry
+
+    row, col = iota((512, 64), 0), iota((512, 64), 1)
+    chosen = (row >> 3) == col
+    s = (iota((512, 1), 0) & 3).astype(f32)
+    source = jnp.where(s < pick(512, chosen, count), pick(512, chosen, offset) + s, -1.0)
+    take = (iota((512, slots), 1).astype(f32) == source).astype(bf16)
+    low = (iota((512, 256), 0) & 7) < 4
+    for c in range(4):
+        quarter = [
+            dot(take, moments[:, q * 1024 + c * 256 : q * 1024 + (c + 1) * 256]) for q in range(4)
+        ]
+        upper = jnp.where(low, quarter[0], quarter[1]).reshape(64, 8, 256)
+        lower = jnp.where(low, quarter[2], quarter[3]).reshape(64, 8, 256)
+        send[:, :, c * 256 : (c + 1) * 256] = jnp.concatenate([upper, lower], axis=1).astype(bf16)
+
+    core_copy.wait()
+    mine = pl.ds(k * 32, 32)
+
+    def add_core(g, carry):
+        part_core[g] = extra[k * 32 + g] + extra_core[g]
+        return carry
+
+    lax.fori_loop(0, 32, add_core, 0)
+
+    def y_copy(dy):
+        to = lax.rem(y + dy, 4)
+        return pltpu.make_async_remote_copy(
+            src_ref=part_core.at[pl.ds(to * 8, 8)],
+            dst_ref=extra_y.at[dy - 1],
+            send_sem=y_ssem.at[dy - 1],
+            recv_sem=y_rsem.at[dy - 1],
+            device_id=(d, z * 8 + to * 2 + k),
+            device_id_type=MESH,
+        )
+
+    def z_copy(dz):
+        to = lax.rem(z + dz, 8)
+        return pltpu.make_async_remote_copy(
+            src_ref=part_y.at[to],
+            dst_ref=extra_z.at[dz - 1],
+            send_sem=z_ssem.at[dz - 1],
+            recv_sem=z_rsem.at[dz - 1],
+            device_id=(d, to * 8 + y * 2 + k),
+            device_id_type=MESH,
+        )
+
+    for dy in range(1, 4):
+        y_copy(dy).start()
+    lax.fori_loop(24, 48, start_main, 0)
+    for dy in range(1, 4):
+        y_copy(dy).wait()
+
+    def add_y(g, carry):
+        part_y[g] = part_core[y * 8 + g] + (extra_y[0, g] + (extra_y[1, g] + extra_y[2, g]))
+        return carry
+
+    lax.fori_loop(0, 8, add_y, 0)
+    for dz in range(1, 8):
+        z_copy(dz).start()
+    lax.fori_loop(48, 64, start_main, 0)
+    lax.fori_loop(1, 24, start_main, 0)
+    lax.fori_loop(1, 64, start_meta, 0)
+
+    recv[0] = send[e]
+    meta_recv[pl.ds(0, 1), :] = meta_send[pl.ds(e, 1), :]
+
+    def wait_meta(i, carry):
+        meta_copy(i).wait()
+        return carry
+
+    lax.fori_loop(1, 64, wait_meta, 0)
+    meta = meta_recv[...]
+
+    heavy = jnp.sum((meta > float(BASE)).astype(f32), axis=0, keepdims=True)
+    heavy = jnp.where(iota((1, 128), 1) >= 64, heavy, 0.0)
+    flag_ref[...] = jnp.broadcast_to(jnp.max(heavy, axis=1, keepdims=True), (8, 128))
+
+    spread = (iota((64, 1024), 0) == (iota((64, 1024), 1) >> 4)).astype(bf16)
+    by_slot = dot(meta.astype(bf16), spread, ((0,), (0,)))[0:8]
+    lane = iota((1, 1024), 1)
+    goal = jnp.sum(
+        jnp.where(iota((8, 1024), 0) == (lane & 3), by_slot, 0.0), axis=0, keepdims=True
+    )
+    owned = 4 * share
+    hit = iota((owned, 1024), 0).astype(f32) + 1.0 == goal
+    for q in range(4):
+        place[q * owned : (q + 1) * owned, :] = jnp.where(
+            jnp.logical_and(hit, ((lane >> 2) & 3) == q), 1.0, 0.0
+        ).astype(bf16)
+    late_goal = jnp.sum(meta, axis=0, keepdims=True)
+    late_lane = iota((owned, 128), 1)
+    late_hit = jnp.logical_and(
+        iota((owned, 128), 0).astype(f32) + 1.0 == late_goal,
+        jnp.logical_and(late_lane >= BASE, late_lane < BASE + EXTRA),
+    )
+    late_place = jnp.where(late_hit, 1.0, 0.0).astype(bf16)[:, :16]
+
+    for dz in range(1, 8):
+        z_copy(dz).wait()
+    late[...] = jnp.zeros_like(late)
+    total = part_y[z].astype(f32)
+    for dz in range(1, 8):
+        total = total + extra_z[dz - 1].astype(f32)
+    late[BASE * 32 : (BASE + EXTRA) * 32, :] = total
+
+    def wait_main(i, carry):
+        main_copy(i).wait()
+        return carry
+
+    lax.fori_loop(1, 64, wait_main, 0)
+    own_grad.wait()
+    for dx in range(1, 4):
+        grad_copy(dx).wait()
+
+    for c in range(4):
+        lanes = slice(c * 256, (c + 1) * 256)
+        arrived = dot(place[...], recv[:, :, lanes].reshape(1024, 256))
+        for q in range(4):
+            block = q * 8 + c * 2
+            rest = jnp.concatenate(
+                [late[pl.ds(block, 16, stride=32), :], late[pl.ds(block + 1, 16, stride=32), :]], axis=1
+            ).astype(bf16)
+            landed[q * owned : (q + 1) * owned, lanes] = arrived[q * owned : (q + 1) * owned] + dot(
+                late_place, rest
+            )
+
+    def update(ex, carry):
+        scale_lane = iota((share, 16), 1)
+        m_scales = jnp.zeros((share, 16), f32)
+        v_scales = jnp.zeros((share, 16), f32)
+        for b in range(16):
+            at = pl.ds(pl.multiple_of(ex * share + (b // 8) * owned, 16), share)
+            at_v = pl.ds(pl.multiple_of(ex * share + (2 + b // 8) * owned, 16), share)
+            lanes = slice((b % 8) * 128, (b % 8 + 1) * 128)
+            out = slice(b * 128, (b + 1) * 128)
+            g = (grads[0, ex, :, out].astype(f32) + grads[1, ex, :, out].astype(f32)) + (
+                grads[2, ex, :, out].astype(f32) + grads[3, ex, :, out].astype(f32)
+            )
+            m = beta_one * landed[at, lanes] + (1.0 - beta_one) * g
+            v = beta_two * landed[at_v, lanes] + (1.0 - beta_two) * g * g
+            dir_ref[ex, :, out] = m / (jnp.sqrt(v) + adam_eps)
+            m_scale = (jnp.max(jnp.abs(m), axis=1, keepdims=True) + scale_eps).astype(bf16)
+            v_scale = (jnp.max(jnp.abs(v), axis=1, keepdims=True) + scale_eps).astype(bf16)
+            m_wide, v_wide = m_scale.astype(f32), v_scale.astype(f32)
+            codes_ref[0, ex, :, out] = (m * (1.0 / m_wide)).astype(bf16)
+            codes_ref[1, ex, :, out] = (v * (1.0 / v_wide)).astype(bf16)
+            m_scales = jnp.where(scale_lane == b, m_wide, m_scales)
+            v_scales = jnp.where(scale_lane == b, v_wide, v_scales)
+        scales_ref[0, ex] = m_scales.astype(bf16)
+        scales_ref[1, ex] = v_scales.astype(bf16)
+        return carry
+
+    lax.fori_loop(0, 4, update, 0)
+
+
+def exchange(grad_parts, m_codes, v_codes, m_scale, v_scale, expert_map, slot_expert, slot_row, count, offset):
+    slots, width, blocks = m_codes.shape[2], m_codes.shape[3], m_scale.shape[3]
+    share = grad_parts.shape[2] // 4
+    owned = 4 * share
+    vmem = pl.BlockSpec(memory_space=pltpu.VMEM)
+    chunk = 32 * EXTRA
+    return pl.pallas_call(
+        resume_kernel,
+        out_shape=(
+            jax.ShapeDtypeStruct((4, share, width), f32),
+            jax.ShapeDtypeStruct((2, 4, share, width), bf16),
+            jax.ShapeDtypeStruct((2, 4, share, blocks), bf16),
+            jax.ShapeDtypeStruct((8, 128), f32),
+        ),
+        in_specs=[pl.BlockSpec(memory_space=pl.ANY)] + [vmem] * 9,
+        out_specs=(vmem,) * 4,
+        scratch_shapes=[
+            pltpu.VMEM((slots, 2 * width), bf16),
+            pltpu.VMEM((64 * chunk, 128), f32),
+            pltpu.VMEM((64, chunk, 128), bf16),
+            pltpu.VMEM((32, chunk, 128), bf16),
+            pltpu.VMEM((3, 8, chunk, 128), bf16),
+            pltpu.VMEM((7, chunk, 128), bf16),
+            pltpu.VMEM((32, chunk, 128), bf16),
+            pltpu.VMEM((8, chunk, 128), bf16),
+            pltpu.VMEM((64, 16, 1024), bf16),
+            pltpu.VMEM((64, 16, 1024), bf16),
+            pltpu.VMEM((64, 128), f32),
+            pltpu.VMEM((64, 128), f32),
+            pltpu.VMEM((4, 4, share, width), bf16),
+            pltpu.VMEM((4 * owned, 1024), bf16),
+            pltpu.VMEM((16 * 32, 128), f32),
+            pltpu.VMEM((4 * owned, 1024), f32),
+            pltpu.SemaphoreType.DMA((64,)),
+            pltpu.SemaphoreType.DMA((64,)),
+            pltpu.SemaphoreType.DMA((64,)),
+            pltpu.SemaphoreType.DMA((64,)),
+            pltpu.SemaphoreType.DMA((4,)),
+            pltpu.SemaphoreType.DMA((4,)),
+            pltpu.SemaphoreType.DMA((2,)),
+            pltpu.SemaphoreType.DMA((3,)),
+            pltpu.SemaphoreType.DMA((3,)),
+            pltpu.SemaphoreType.DMA((7,)),
+            pltpu.SemaphoreType.DMA((7,)),
+        ],
+        compiler_params=pltpu.CompilerParams(
+            collective_id=0, has_side_effects=True, vmem_limit_bytes=56 * 2**20
+        ),
+        name="resume",
+    )(
+        grad_parts,
+        m_codes[0, 0],
+        v_codes[0, 0],
+        m_scale[0, 0],
+        v_scale[0, 0],
+        expert_map.reshape(1, -1),
+        slot_expert,
+        slot_row,
+        count,
+        offset,
+    )
+
+
+def per_device(*args):
+    direction, codes, scales, heavy = exchange(*args)
+    return lax.cond(
+        heavy[0, 0] < 1.5,
+        lambda: (direction, codes, scales),
+        lambda: padded_exchange(*args),
+    )
+
+
 def solution(mesh):
     in_specs = (
         P("dp", "expert", None, None),

time: 317 us -> 113 us (0.36)
  waiting for transfers between devices: 141 us -> 0 us
  Pallas kernels: 0 us -> 89.3 us
  local copies, waits for them, and re-layouts: 93.6 us -> 8.31 us
  other arithmetic: 35.4 us -> 0 us
  starting transfers between devices: 31.1 us -> 0 us
    all_to_all x3 -> x0, waiting for transfers between devices: 140 us -> none  [the longest x1 77.7 us: per_device(): lax.all_to_all(sent_first.astype(jnp.bfloat16), 'expert', split_axis=0, c...]
    pallas_call x0 -> x1, Pallas kernels: none -> 89.3 us  [exchange(): pl.pallas_call(resume_kernel, out_shape=(jax.ShapeDtypeStruct((4, share,...]
    all_to_all x3 -> x0, starting transfers between devices: 31 us -> none  [the longest x1 13.2 us: per_device(): lax.all_to_all(targets, 'expert', split_axis=0, concat_axis=0, tiled=True)]
    convert_element_type x5 -> x0, other arithmetic: 23.2 us -> none  [the longest x1 9.36 us: per_device(): sent_first.astype(jnp.bfloat16)]
    scatter x2 -> x0, local copies, waits for them, and re-layouts: 20.7 us -> none  [the longest x1 10.4 us: per_device(): first_moment = jnp.zeros((owned_rows, width), jnp.float32).at[landing].se...]
    mul x4 -> x0, local copies, waits for them, and re-layouts: 20.4 us -> none  [dequantize(): blocks * block_scale.astype(jnp.float32)[..., None]]
    gather x6 -> x0, local copies, waits for them, and re-layouts: 18.5 us -> none  [the longest x1 4.08 us: per_device(): codes_first[picked]]
    convert_element_type x4 -> x0, local copies, waits for them, and re-layouts: 11.5 us -> none  [the longest x2 11.4 us: dequantize(): code_array.astype(jnp.float32)]
  transfers between devices with their start and end apart: 4 -> 0, of which waited for: 2 -> 0; matrix products, arithmetic and copies ran while one was open for 31% -> 0% of each run, Pallas kernels for 0% -> 0%
where the time goes in v1:
time: 113 us
  Pallas kernels  89.3 us (79%)
  between operations  14.8 us (13%)
  local copies, waits for them, and re-layouts  8.31 us (7%)
    pallas_call x1, Pallas kernels, exchange(): pl.pallas_call(resume_kernel, out_shape=(jax.ShapeDtypeStruct((4, share,...  89.3 us
    unnamed x24, local copies, waits for them, and re-layouts  7.03 us

profile of v1, /device:TPU:1, one launch (start us, length us, event | category | flops | bytes accessed | tf_op | source)
XLA Modules:
  0.0 112.6 jit_solution(1320412342899049341)
XLA Ops:
  7.2 1.5 %copy.45 = bf16[1,1,576,16]{3,2,1,0:T(8,128)(2,1)} copy(bf16[1,1,576,16]{2,3,1,0:T(8,128)(2,1)} %param.15) | data formatting | bytes 36864 | tf_op args[3]
  8.7 1.5 %copy.46 = bf16[1,1,576,16]{3,2,1,0:T(8,128)(2,1)} copy(bf16[1,1,576,16]{2,3,1,0:T(8,128)(2,1)} %param.16) | data formatting | bytes 36864 | tf_op args[4]
  10.2 0.0 copy-start.7
  10.2 0.0 copy-start.8
  10.2 0.0 copy-start.9
  10.2 0.0 copy-start.10
  10.2 89.3 %resume.1 = (f32[4,48,2048]{2,1,0:T(8,128)}, bf16[2,4,48,2048]{3,2,1,0:T(8,128)(2,1)}, bf16[2,4,48,16]{3,2,1,0:T(8,128)(2,1)S(1)}, f32[8,128]{1,0:T(8,128)}) custom-call(bf16[1,4,192,2048]{3,2,1,0:T(8,128)(2,1)} %grad_ref.1, bf16[576,2048]{1,0:T(8,128)(2,1)} %bitcast.43, bf16[576,2048]{1,0:T(8,128)(2,1)} %bitcast.45, bf16[576,16]{1,0:T(8,128)(2,1)} %bitcast.58, ...), custom_call_target="tpu_custom_call" | custom-call | tf_op jit(solution)/shard_map/resume/pallas_call | solution.py:469
  99.5 1.2 %slice.3 = f32[1,1]{1,0:T(1,128)} slice(f32[8,128]{1,0:T(8,128)} %get-tuple-element.43), slice={[0:1], [0:1]} | slice | bytes 8 | tf_op jit(solution)/shard_map/slice | solution.py:529
  101.4 0.0 copy-done
  101.4 0.0 copy-done.1
  101.4 0.0 copy-done.4
  101.4 0.0 copy-done.5
  101.4 0.0 copy-done.7
  101.4 0.0 copy-done.8
  101.4 0.0 copy-done.9
  101.4 0.0 copy-done.10
  101.4 0.3 conditional.1
  101.7 0.1 copy.49
  101.8 0.0 copy-start.6
  101.8 0.0 copy-start.3
  101.8 2.8 %copy.60 = f32[4,48,2048]{2,1,0:T(8,128)} copy(f32[4,48,2048]{2,1,0:T(8,128)} %get-tuple-element.136) | data formatting | bytes 3145728
  104.6 0.0 copy-done.6
  104.6 0.0 copy-done.3
  104.6 1.1 %copy.61 = bf16[2,4,48,2048]{3,2,1,0:T(8,128)(2,1)} copy(bf16[2,4,48,2048]{3,2,1,0:T(8,128)(2,1)S(1)} %copy-done.3) | data formatting | bytes 3145728
  (4 shorter events, 0.0 us)
Async XLA Ops:
  10.2 91.2 %copy-start = (s32[256]{0:T(256)S(1)}, s32[256]{0:T(256)}, u32[]{:S(2)}) copy-start(s32[256]{0:T(256)} %param.17) | copy-start | bytes 3076
  10.2 91.2 %copy-start.1 = (bf16[1,1,576,2048]{3,2,1,0:T(8,128)(2,1)S(1)}, bf16[1,1,576,2048]{3,2,1,0:T(8,128)(2,1)}, u32[]{:S(2)}) copy-start(bf16[1,1,576,2048]{3,2,1,0:T(8,128)(2,1)} %param.13) | copy-start | bytes 7077892
  10.2 91.2 %copy-start.4 = (bf16[1,1,576,16]{2,3,1,0:T(8,128)(2,1)S(1)}, bf16[1,1,576,16]{2,3,1,0:T(8,128)(2,1)}, u32[]{:S(2)}) copy-start(bf16[1,1,576,16]{2,3,1,0:T(8,128)(2,1)} %param.15) | copy-start | bytes 55300
  10.2 91.2 %copy-start.5 = (bf16[1,1,576,16]{2,3,1,0:T(8,128)(2,1)S(1)}, bf16[1,1,576,16]{2,3,1,0:T(8,128)(2,1)}, u32[]{:S(2)}) copy-start(bf16[1,1,576,16]{2,3,1,0:T(8,128)(2,1)} %param.16) | copy-start | bytes 55300
  10.2 91.2 %copy-start.7 = (s32[1,576]{1,0:T(1,128)S(1)}, s32[1,576]{1,0:T(1,128)}, u32[]{:S(2)}) copy-start(s32[1,576]{1,0:T(1,128)} %row_ref.1) | copy-start | bytes 6916
  10.2 91.2 %copy-start.8 = (s32[1,576]{1,0:T(1,128)S(1)}, s32[1,576]{1,0:T(1,128)}, u32[]{:S(2)}) copy-start(s32[1,576]{1,0:T(1,128)} %expert_ref.1) | copy-start | bytes 6916
  10.2 91.2 %copy-start.9 = (s32[1,64]{1,0:T(1,128)S(1)}, s32[1,64]{1,0:T(1,128)}, u32[]{:S(2)}) copy-start(s32[1,64]{1,0:T(1,128)} %count_ref.1) | copy-start | bytes 772
  10.2 91.2 %copy-start.10 = (s32[1,64]{1,0:T(1,128)S(1)}, s32[1,64]{1,0:T(1,128)}, u32[]{:S(2)}) copy-start(s32[1,64]{1,0:T(1,128)} %offset_ref.1) | copy-start | bytes 772
  101.8 2.8 %copy-start.6 = (bf16[2,4,48,16]{2,3,1,0:T(8,128)(2,1)}, bf16[2,4,48,16]{2,3,1,0:T(8,128)(2,1)S(1)}, u32[]{:S(2)}) copy-start(bf16[2,4,48,16]{2,3,1,0:T(8,128)(2,1)S(1)} %get-tuple-element.138) | copy-start | bytes 36868
  101.8 2.8 %copy-start.3 = (bf16[2,4,48,2048]{3,2,1,0:T(8,128)(2,1)S(1)}, bf16[2,4,48,2048]{3,2,1,0:T(8,128)(2,1)}, u32[]{:S(2)}) copy-start(bf16[2,4,48,2048]{3,2,1,0:T(8,128)(2,1)} %get-tuple-element.137) | copy-start | bytes 4718596

commit v2 on v1

v2 whole, which is shorter than its diff:
```python
import functools

import jax
import jax.numpy as jnp
from jax import lax
from jax.experimental import pallas as pl
from jax.experimental.pallas import tpu as pltpu
from jax.sharding import PartitionSpec as P

beta_one = 0.9
beta_two = 0.95
adam_eps = 1e-08
scale_eps = 1e-06

MESH = pl.DeviceIdType.MESH
f32 = jnp.float32
bf16 = jnp.bfloat16
BASE = 4
EXTRA = 5
VMEM_MIB = 44


def dequantize(code_array, block_scale):
    full_shape = code_array.shape
    blocks = code_array.astype(jnp.float32).reshape(
        full_shape[:-1] + (block_scale.shape[-1], full_shape[-1] // block_scale.shape[-1])
    )
    return (blocks * block_scale.astype(jnp.float32)[..., None]).reshape(full_shape)


def quantize(values, block_count):
    full_shape = values.shape
    blocks = values.reshape(full_shape[:-1] + (block_count, full_shape[-1] // block_count))
    block_scale = (jnp.max(jnp.abs(blocks), axis=-1) + scale_eps).astype(jnp.bfloat16)
    code_array = (blocks / block_scale.astype(jnp.float32)[..., None]).astype(jnp.bfloat16)
    return (code_array.reshape(full_shape), block_scale)


def padded_exchange(
    grad_parts,
    old_m_codes,
    old_v_codes,
    old_m_scale,
    old_v_scale,
    expert_map,
    slot_expert,
    slot_row,
    peer_count,
    peer_offset,
):
    owners = lax.axis_size("expert")
    codes_first = old_m_codes[0, 0]
    codes_second = old_v_codes[0, 0]
    scale_first = old_m_scale[0, 0]
    scale_second = old_v_scale[0, 0]
    slot_total = codes_first.shape[0]
    width = codes_first.shape[1]
    block_count = scale_first.shape[1]
    per_peer = slot_total // owners
    exp_dev = grad_parts.shape[1]
    share_rows = grad_parts.shape[2] // lax.axis_size("dp")
    owned_rows = exp_dev * share_rows
    send_counts = peer_count[0]
    offsets = peer_offset[0]
    slot_place = jnp.arange(per_peer, dtype=jnp.int32)[None, :]
    picked = (offsets[:, None] + slot_place).reshape(-1)
    new_expert = expert_map[slot_expert[0]]
    local_all = new_expert % exp_dev * share_rows + slot_row[0]
    usable = slot_place < send_counts[:, None]
    targets = jnp.where(usable, local_all[picked].reshape(owners, per_peer), -1)
    arrived_targets = lax.all_to_all(targets, "expert", split_axis=0, concat_axis=0, tiled=True)
    sent_first = dequantize(codes_first[picked], scale_first[picked]).reshape(
        owners, per_peer, width
    )
    sent_second = dequantize(codes_second[picked], scale_second[picked]).reshape(
        owners, per_peer, width
    )
    first_rows = lax.all_to_all(
        sent_first.astype(jnp.bfloat16), "expert", split_axis=0, concat_axis=0, tiled=True
    ).astype(sent_first.dtype)
    second_rows = lax.all_to_all(
        sent_second.astype(jnp.bfloat16), "expert", split_axis=0, concat_axis=0, tiled=True
    ).astype(sent_second.dtype)
    flat_targets = arrived_targets.reshape(-1)
    landing = jnp.where(flat_targets >= 0, flat_targets, owned_rows)
    first_moment = (
        jnp.zeros((owned_rows, width), jnp.float32)
        .at[landing]
        .set(first_rows.reshape(-1, width), mode="drop")
    )
    second_moment = (
        jnp.zeros((owned_rows, width), jnp.float32)
        .at[landing]
        .set(second_rows.reshape(-1, width), mode="drop")
    )
    first_moment, second_moment = (
        first_moment.reshape(exp_dev, share_rows, width),
        second_moment.reshape(exp_dev, share_rows, width),
    )
    replicas = lax.axis_size("dp")
    grad_terms = grad_parts[0].reshape(exp_dev, replicas, share_rows, width)
    grad_terms = lax.all_to_all(grad_terms, "dp", split_axis=1, concat_axis=1, tiled=True)
    grad_share = jnp.sum(grad_terms.astype(jnp.float32), axis=1)
    first_new = beta_one * first_moment + (1.0 - beta_one) * grad_share
    second_new = beta_two * second_moment + (1.0 - beta_two) * grad_share * grad_share
    direction = first_new / (jnp.sqrt(second_new) + adam_eps)
    code_first, new_scale_first = quantize(first_new, block_count)
    code_second, new_scale_second = quantize(second_new, block_count)
    return (
        direction,
        jnp.stack([code_first, code_second]),
        jnp.stack([new_scale_first, new_scale_second]),
    )


def iota(shape, dim):
    return lax.broadcasted_iota(jnp.int32, shape, dim)


def dot(a, b, dims=((1,), (0,))):
    return lax.dot_general(a, b, (dims, ((), ())), preferred_element_type=f32)


def pick(rows, chosen, vector):
    return jnp.sum(jnp.where(chosen, vector, 0.0), axis=1, keepdims=True)


def resume_kernel(
    grad_ref,
    m_ref,
    v_ref,
    ms_ref,
    vs_ref,
    map_ref,
    expert_ref,
    row_ref,
    count_ref,
    offset_ref,
    dir_ref,
    codes_ref,
    scales_ref,
    flag_ref,
    old,
    moments,
    relay,
    extra,
    extra_core,
    extra_y,
    extra_z,
    part_core,
    part_y,
    send,
    recv,
    meta_send,
    meta_recv,
    grads,
    total_grad,
    place,
    late,
    wide_scales,
    load_sem,
    send_sem,
    recv_sem,
    meta_ssem,
    meta_rsem,
    grad_ssem,
    grad_rsem,
    core_sem,
    y_ssem,
    y_rsem,
    z_ssem,
    z_rsem,
):
    d = lax.axis_index("dp")
    e = lax.axis_index("expert")
    z, y, k = lax.div(e, 8), lax.rem(lax.div(e, 2), 4), lax.rem(e, 2)
    share = grads.shape[2]
    owned = 4 * share
    slots = old.shape[0]

    def peer(i):
        pz = lax.rem(z + lax.div(i, 8), 8)
        py = lax.rem(y + lax.rem(lax.div(i, 2), 4), 4)
        pk = lax.rem(k + lax.rem(i, 2), 2)
        return pz * 8 + py * 2 + pk

    def load(p, q):
        source = (m_ref, v_ref)[q // 2]
        return pltpu.make_async_copy(
            source.at[:, pl.ds((q % 2) * 1024 + p * 512, 512)],
            old.at[:, pl.ds(q * 1024 + p * 512, 512)],
            load_sem.at[p * 4 + q],
        )

    for p in range(2):
        for q in range(4):
            load(p, q).start()

    barrier = pltpu.get_barrier_semaphore()

    def greet(i, carry):
        pl.semaphore_signal(barrier, inc=1, device_id=(d, peer(i)), device_id_type=MESH)
        return carry

    for dx in range(1, 4):
        pl.semaphore_signal(
            barrier, inc=1, device_id=(lax.rem(d + dx, 4), e), device_id_type=MESH
        )
    lax.fori_loop(1, 64, greet, 0)

    count = count_ref[...].astype(f32)
    offset = offset_ref[...].astype(f32)
    unit = (iota((16, 16), 0) == iota((16, 16), 1)).astype(bf16)
    columns = (dot(ms_ref[...], unit, ((0,), (0,))), dot(vs_ref[...], unit, ((0,), (0,))))

    row, col = iota((512, 64), 0), iota((512, 64), 1)
    chosen = (row >> 3) == col
    s = (iota((512, 1), 0) & 3).astype(f32)
    source = jnp.where(s < pick(512, chosen, count), pick(512, chosen, offset) + s, -1.0)
    take = (iota((512, slots), 1).astype(f32) == source).astype(bf16)
    low = (iota((512, 256), 0) & 7) < 4

    def dequantize_half(p):
        for q in range(4):
            load(p, q).wait()
        for q in range(4):
            for b in range(4):
                block = (q % 2) * 8 + p * 4 + b
                lanes = slice(q * 1024 + p * 512 + b * 128, q * 1024 + p * 512 + (b + 1) * 128)
                moments[:, lanes] = (
                    old[:, lanes].astype(f32) * columns[q // 2][:, block : block + 1]
                ).astype(bf16)

    def pack(p):
        for c in range(2 * p, 2 * p + 2):
            quarter = [
                dot(take, moments[:, q * 1024 + c * 256 : q * 1024 + (c + 1) * 256])
                for q in range(4)
            ]
            upper = jnp.where(low, quarter[0], quarter[1]).reshape(64, 8, 256)
            lower = jnp.where(low, quarter[2], quarter[3]).reshape(64, 8, 256)
            send[p, :, :, (c % 2) * 256 : (c % 2 + 1) * 256] = jnp.concatenate(
                [upper, lower], axis=1
            ).astype(bf16)

    dequantize_half(0)
    pack(0)

    pl.semaphore_wait(barrier, 66)

    def grad_copy(dx):
        to = lax.rem(d + dx, 4)
        return pltpu.make_async_remote_copy(
            src_ref=grad_ref.at[0, :, pl.ds(pl.multiple_of(to * share, 16), share), :],
            dst_ref=grads.at[dx],
            send_sem=grad_ssem.at[dx],
            recv_sem=grad_rsem.at[dx],
            device_id=(to, e),
            device_id_type=MESH,
        )

    own_grad = pltpu.make_async_copy(
        grad_ref.at[0, :, pl.ds(pl.multiple_of(d * share, 16), share), :], grads.at[0], grad_ssem.at[0]
    )

    def meta_copy(i):
        to = peer(i)
        return pltpu.make_async_remote_copy(
            src_ref=meta_send.at[pl.ds(to, 1)],
            dst_ref=meta_recv.at[pl.ds(i, 1)],
            send_sem=meta_ssem.at[i],
            recv_sem=meta_rsem.at[i],
            device_id=(d, to),
            device_id_type=MESH,
        )

    def main_copy(p, i):
        to = peer(i)
        return pltpu.make_async_remote_copy(
            src_ref=send.at[p, to],
            dst_ref=recv.at[p, i],
            send_sem=send_sem.at[p, i],
            recv_sem=recv_sem.at[p, i],
            device_id=(d, to),
            device_id_type=MESH,
        )

    def start_meta(i, carry):
        meta_copy(i).start()
        return carry

    def wait_meta(i, carry):
        meta_copy(i).wait()
        return carry

    def start_main(p):
        def start(i, carry):
            main_copy(p, i).start()
            return carry

        return start

    def wait_main(p):
        def wait(i, carry):
            main_copy(p, i).wait()
            return carry

        return wait

    for dx in range(1, 4):
        grad_copy(dx).start()
    own_grad.start()
    lax.fori_loop(24, 64, start_main(0), 0)
    lax.fori_loop(1, 24, start_main(0), 0)
    recv[0, 0] = send[0, e]

    dequantize_half(1)
    row, col = iota((64 * EXTRA, 64), 0), iota((64 * EXTRA, 64), 1)
    u = row & 63
    owner = ((u & 7) << 3) | (((u >> 3) & 3) << 1) | (u >> 5)
    chosen = owner == col
    s = (iota((64 * EXTRA, 1), 0) >> 6).astype(f32) + float(BASE)
    source = jnp.where(
        s < pick(64 * EXTRA, chosen, count), pick(64 * EXTRA, chosen, offset) + s, -1.0
    )
    take_extra = (iota((64 * EXTRA, slots), 1).astype(f32) == source).astype(bf16)
    for c in range(8):
        rows = dot(take_extra, moments[:, c * 512 : (c + 1) * 512])
        for s_i in range(EXTRA):
            for q in range(4):
                relay[pl.ds(s_i * 32 + c * 4 + q, 64, stride=32 * EXTRA), :] = rows[
                    s_i * 64 : (s_i + 1) * 64, q * 128 : (q + 1) * 128
                ]

    def narrow(u, carry):
        extra[u] = relay[pl.ds(pl.multiple_of(u * 32 * EXTRA, 32), 32 * EXTRA), :].astype(bf16)
        return carry

    lax.fori_loop(0, 64, narrow, 0)

    core_copy = pltpu.make_async_remote_copy(
        src_ref=extra.at[pl.ds((1 - k) * 32, 32)],
        dst_ref=extra_core,
        send_sem=core_sem.at[0],
        recv_sem=core_sem.at[1],
        device_id=(d, peer(1)),
        device_id_type=MESH,
    )
    core_copy.start()
    pack(1)
    core_copy.wait()

    def add_core(g, carry):
        part_core[g] = extra[k * 32 + g] + extra_core[g]
        return carry

    lax.fori_loop(0, 32, add_core, 0)

    def y_copy(dy):
        to = lax.rem(y + dy, 4)
        return pltpu.make_async_remote_copy(
            src_ref=part_core.at[pl.ds(to * 8, 8)],
            dst_ref=extra_y.at[dy - 1],
            send_sem=y_ssem.at[dy - 1],
            recv_sem=y_rsem.at[dy - 1],
            device_id=(d, z * 8 + to * 2 + k),
            device_id_type=MESH,
        )

    def z_copy(dz):
        to = lax.rem(z + dz, 8)
        return pltpu.make_async_remote_copy(
            src_ref=part_y.at[to],
            dst_ref=extra_z.at[dz - 1],
            send_sem=z_ssem.at[dz - 1],
            recv_sem=z_rsem.at[dz - 1],
            device_id=(d, to * 8 + y * 2 + k),
            device_id_type=MESH,
        )

    for dy in range(1, 4):
        y_copy(dy).start()
    lax.fori_loop(24, 48, start_main(1), 0)

    orow, ocol = iota((64, 64), 0), iota((64, 64), 1)
    count_col = pick(64, orow == ocol, count)
    offset_col = pick(64, orow == ocol, offset)
    lane = iota((64, slots), 1).astype(f32)
    held = jnp.logical_and(lane >= offset_col, lane < offset_col + count_col)
    rank = iota((1, slots), 1).astype(f32) - jnp.sum(
        jnp.where(held, offset_col, 0.0), axis=0, keepdims=True
    )
    old_place = iota((256, slots), 0) == expert_ref[...]
    mapped = dot(
        jnp.broadcast_to(map_ref[...].astype(f32), (8, 256)).astype(bf16), old_place.astype(bf16)
    )[0:1]
    land = (mapped - 4.0 * jnp.floor(mapped * 0.25)) * float(share) + row_ref[...].astype(f32) + 1.0
    held_land = jnp.where(held, land, 0.0).astype(bf16)
    at_rank = (iota((128, slots), 0).astype(f32) == rank).astype(bf16)
    targets = dot(held_land, at_rank, ((1,), (1,)))
    shift = (iota((64, 128), 0) + 64 == iota((64, 128), 1)).astype(bf16)
    counts = dot(jnp.broadcast_to(count, (64, 64)).astype(bf16), shift)
    meta_send[...] = jnp.where(iota((64, 128), 1) < 16, targets, counts)

    for dy in range(1, 4):
        y_copy(dy).wait()

    def add_y(g, carry):
        part_y[g] = part_core[y * 8 + g] + (extra_y[0, g] + (extra_y[1, g] + extra_y[2, g]))
        return carry

    lax.fori_loop(0, 8, add_y, 0)
    for dz in range(1, 8):
        z_copy(dz).start()
    lax.fori_loop(48, 64, start_main(1), 0)
    lax.fori_loop(1, 24, start_main(1), 0)
    lax.fori_loop(1, 64, start_meta, 0)

    recv[1, 0] = send[1, e]
    meta_recv[pl.ds(0, 1), :] = meta_send[pl.ds(e, 1), :]

    own_grad.wait()
    for dx in range(1, 4):
        grad_copy(dx).wait()
    for ex in range(4):
        total_grad[ex] = (grads[0, ex].astype(f32) + grads[1, ex].astype(f32)) + (
            grads[2, ex].astype(f32) + grads[3, ex].astype(f32)
        )

    lax.fori_loop(1, 64, wait_meta, 0)
    meta = meta_recv[...]

    heavy = jnp.sum((meta > float(BASE)).astype(f32), axis=0, keepdims=True)
    heavy = jnp.where(iota((1, 128), 1) >= 64, heavy, 0.0)
    flag_ref[0] = jnp.max(heavy).astype(jnp.int32)

    spread = (iota((64, 1024), 0) == (iota((64, 1024), 1) >> 4)).astype(bf16)
    by_slot = dot(meta.astype(bf16), spread, ((0,), (0,)))[0:8]
    lane = iota((1, 1024), 1)
    goal = jnp.sum(
        jnp.where(iota((8, 1024), 0) == (lane & 3), by_slot, 0.0), axis=0, keepdims=True
    )
    hit = iota((owned, 1024), 0).astype(f32) + 1.0 == goal
    for q in range(4):
        place[q * owned : (q + 1) * owned, :] = jnp.where(
            jnp.logical_and(hit, ((lane >> 2) & 3) == q), 1.0, 0.0
        ).astype(bf16)
    late_goal = jnp.sum(meta, axis=0, keepdims=True)
    late_lane = iota((owned, 128), 1)
    late_hit = jnp.logical_and(
        iota((owned, 128), 0).astype(f32) + 1.0 == late_goal,
        jnp.logical_and(late_lane >= BASE, late_lane < BASE + EXTRA),
    )
    late_place = jnp.where(late_hit, 1.0, 0.0).astype(bf16)[:, :16]

    for dz in range(1, 8):
        z_copy(dz).wait()
    late[...] = jnp.zeros_like(late)
    total = part_y[z].astype(f32)
    for dz in range(1, 8):
        total = total + extra_z[dz - 1].astype(f32)
    late[BASE * 32 : (BASE + EXTRA) * 32, :] = total

    def unpack(p):
        for c in range(2):
            arrived = dot(
                place[...], recv[p, :, :, c * 256 : (c + 1) * 256].reshape(1024, 256)
            )
            for q in range(4):
                for b in range(2):
                    block = p * 4 + c * 2 + b
                    rest = late[pl.ds(q * 8 + block, 16, stride=32), :].astype(bf16)
                    relay[(q * 8 + block) * owned : (q * 8 + block + 1) * owned, :] = arrived[
                        q * owned : (q + 1) * owned, b * 128 : (b + 1) * 128
                    ] + dot(late_place, rest)

    def update(p):
        def one(ex, carry):
            scale_lane = iota((share, 16), 1)
            m_scales = wide_scales[0, ex]
            v_scales = wide_scales[1, ex]
            for b in [h * 8 + p * 4 + i for h in range(2) for i in range(4)]:
                at = pl.ds(pl.multiple_of(ex * share, 16) + b * owned, share)
                at_v = pl.ds(pl.multiple_of(ex * share, 16) + (16 + b) * owned, share)
                out = slice(b * 128, (b + 1) * 128)
                g = total_grad[ex, :, out]
                m = beta_one * relay[at, :] + (1.0 - beta_one) * g
                v = beta_two * relay[at_v, :] + (1.0 - beta_two) * g * g
                dir_ref[ex, :, out] = m / (jnp.sqrt(v) + adam_eps)
                m_scale = (jnp.max(jnp.abs(m), axis=1, keepdims=True) + scale_eps).astype(bf16)
                v_scale = (jnp.max(jnp.abs(v), axis=1, keepdims=True) + scale_eps).astype(bf16)
                m_wide, v_wide = m_scale.astype(f32), v_scale.astype(f32)
                codes_ref[0, ex, :, out] = (m * (1.0 / m_wide)).astype(bf16)
                codes_ref[1, ex, :, out] = (v * (1.0 / v_wide)).astype(bf16)
                m_scales = jnp.where(scale_lane == b, m_wide, m_scales)
                v_scales = jnp.where(scale_lane == b, v_wide, v_scales)
            wide_scales[0, ex] = m_scales
            wide_scales[1, ex] = v_scales
            return carry

        lax.fori_loop(0, 4, one, 0)

    wide_scales[...] = jnp.zeros_like(wide_scales)
    lax.fori_loop(1, 64, wait_main(0), 0)
    unpack(0)
    update(0)
    lax.fori_loop(1, 64, wait_main(1), 0)
    unpack(1)
    update(1)
    turn = (iota((share, share), 0) == iota((share, share), 1)).astype(bf16)
    for part in range(2):
        for ex in range(4):
            scales_ref[part, ex] = dot(
                wide_scales[part, ex].astype(bf16), turn, ((0,), (0,))
            ).astype(bf16)


def exchange(grad_parts, m_codes, v_codes, m_scale, v_scale, expert_map, slot_expert, slot_row, count, offset):
    slots, width, blocks = m_codes.shape[2], m_codes.shape[3], m_scale.shape[3]
    share = grad_parts.shape[2] // 4
    owned = 4 * share
    vmem = pl.BlockSpec(memory_space=pltpu.VMEM)
    hbm = pl.BlockSpec(memory_space=pl.ANY)
    chunk = 32 * EXTRA
    direction, codes, scales, heavy = pl.pallas_call(
        resume_kernel,
        out_shape=(
            jax.ShapeDtypeStruct((4, share, width), f32),
            jax.ShapeDtypeStruct((2, 4, share, width), bf16),
            jax.ShapeDtypeStruct((2, 4, blocks, share), bf16),
            jax.ShapeDtypeStruct((1,), jnp.int32),
        ),
        in_specs=[hbm] * 3 + [vmem] * 7,
        out_specs=(vmem,) * 3 + (pl.BlockSpec(memory_space=pltpu.SMEM),),
        scratch_shapes=[
            pltpu.VMEM((slots, 2 * width), bf16),
            pltpu.VMEM((slots, 2 * width), bf16),
            pltpu.VMEM((64 * chunk, 128), f32),
            pltpu.VMEM((64, chunk, 128), bf16),
            pltpu.VMEM((32, chunk, 128), bf16),
            pltpu.VMEM((3, 8, chunk, 128), bf16),
            pltpu.VMEM((7, chunk, 128), bf16),
            pltpu.VMEM((32, chunk, 128), bf16),
            pltpu.VMEM((8, chunk, 128), bf16),
            pltpu.VMEM((2, 64, 16, 512), bf16),
            pltpu.VMEM((2, 64, 16, 512), bf16),
            pltpu.VMEM((64, 128), f32),
            pltpu.VMEM((64, 128), f32),
            pltpu.VMEM((4, 4, share, width), bf16),
            pltpu.VMEM((4, share, width), f32),
            pltpu.VMEM((4 * owned, 1024), bf16),
            pltpu.VMEM((16 * 32, 128), f32),
            pltpu.VMEM((2, 4, share, 16), f32),
            pltpu.SemaphoreType.DMA((8,)),
            pltpu.SemaphoreType.DMA((2, 64)),
            pltpu.SemaphoreType.DMA((2, 64)),
            pltpu.SemaphoreType.DMA((64,)),
            pltpu.SemaphoreType.DMA((64,)),
            pltpu.SemaphoreType.DMA((4,)),
            pltpu.SemaphoreType.DMA((4,)),
            pltpu.SemaphoreType.DMA((2,)),
            pltpu.SemaphoreType.DMA((3,)),
            pltpu.SemaphoreType.DMA((3,)),
            pltpu.SemaphoreType.DMA((7,)),
            pltpu.SemaphoreType.DMA((7,)),
        ],
        compiler_params=pltpu.CompilerParams(
            collective_id=0, has_side_effects=True, vmem_limit_bytes=VMEM_MIB * 2**20
        ),
        name="resume",
    )(
        grad_parts,
        m_codes[0, 0],
        v_codes[0, 0],
        m_scale[0, 0].T,
        v_scale[0, 0].T,
        expert_map.reshape(1, -1),
        slot_expert,
        slot_row,
        count,
        offset,
    )
    return direction, codes, jnp.swapaxes(scales, 2, 3), heavy


def per_device(*args):
    direction, codes, scales, heavy = exchange(*args)
    return lax.cond(
        heavy[0] < 2,
        lambda: (direction, codes, scales),
        lambda: padded_exchange(*args),
    )


def solution(mesh):
    in_specs = (
        P("dp", "expert", None, None),
        P("dp", "expert", None, None),
        P("dp", "expert", None, None),
        P("dp", "expert", None, None),
        P("dp", "expert", None, None),
        P(),
        P("expert", None),
        P("expert", None),
        P("expert", None),
        P("expert", None),
    )
    out_specs = (
        P("expert", "dp", None),
        P(None, "expert", "dp", None),
        P(None, "expert", "dp", None),
    )
    return jax.shard_map(
        per_device, mesh=mesh, in_specs=in_specs, out_specs=out_specs, check_vma=False
    )
```

time: 113 us -> 89.3 us (0.79)
  between operations: 14.8 us -> 1.42 us
  Pallas kernels: 89.3 us -> 82.9 us
  local copies, waits for them, and re-layouts: 8.31 us -> 4.61 us
    pallas_call x1, Pallas kernels: 89.3 us -> 82.9 us  [exchange(): pl.pallas_call(resume_kernel, out_shape=(jax.ShapeDtypeStruct((4, share,...]
    unnamed x24 -> x21, local copies, waits for them, and re-layouts: 7.03 us -> 4.61 us
    slice x1 -> x0, local copies, waits for them, and re-layouts: 1.18 us -> none  [per_device(): heavy[0, 0] < 1.5]
where the time goes in v2:
time: 89.3 us; the launch traced here: 89.2 us
  Pallas kernels  82.9 us (93%)
  local copies, waits for them, and re-layouts  4.61 us (5%)
  between operations  1.42 us (2%)
    pallas_call x1, Pallas kernels, exchange(): pl.pallas_call(resume_kernel, out_shape=(jax.ShapeDtypeStruct((4, share,...  82.9 us
    unnamed x21, local copies, waits for them, and re-layouts  4.61 us

profile of v2, /device:TPU:1, one launch (start us, length us, event | category | flops | bytes accessed | tf_op | source)
XLA Modules:
  0.0 89.2 jit_solution(9367903212807004759)
XLA Ops:
  0.6 0.0 copy-start
  0.6 0.0 copy-start.1
  0.7 0.0 copy-start.7
  0.7 0.0 copy-start.8
  0.7 0.0 copy-start.9
  0.7 0.0 copy-start.10
  0.7 0.0 copy-start.11
  0.7 0.0 copy-start.12
  0.7 82.9 %resume.1 = (f32[4,48,2048]{2,1,0:T(8,128)}, bf16[2,4,48,2048]{3,2,1,0:T(8,128)(2,1)}, bf16[2,4,16,48]{3,2,1,0:T(8,128)(2,1)S(1)}, s32[1]{0:T(128)}) custom-call(bf16[1,4,192,2048]{3,2,1,0:T(8,128)(2,1)} %grad_ref.1, bf16[576,2048]{1,0:T(8,128)(2,1)} %bitcast.69, bf16[576,2048]{1,0:T(8,128)(2,1)} %bitcast.71, bf16[16,576]{1,0:T(8,128)(2,1)} %bitcast.84, ...), custom_call_target="tpu_custom_call" | custom-call | tf_op jit(solution)/shard_map/resume/pallas_call | solution.py:525
  84.2 0.0 copy-done
  84.2 0.0 copy-done.1
  84.2 0.0 copy-done.7
  84.2 0.0 copy-done.8
  84.3 0.0 copy-done.9
  84.3 0.0 copy-done.10
  84.3 0.0 copy-done.11
  84.3 0.0 copy-done.12
  84.3 0.3 conditional.1
  84.6 0.0 copy-start.6
  84.6 2.8 %copy.60 = f32[4,48,2048]{2,1,0:T(8,128)} copy(f32[4,48,2048]{2,1,0:T(8,128)} %get-tuple-element.154) | data formatting | bytes 3145728
  87.4 0.0 copy-done.6
  87.4 1.1 %copy.61 = bf16[2,4,48,2048]{3,2,1,0:T(8,128)(2,1)} copy(bf16[2,4,48,2048]{3,2,1,0:T(8,128)(2,1)S(1)} %copy-done.6) | data formatting | bytes 3145728
  88.5 0.6 copy.62
Async XLA Ops:
  0.6 83.6 %copy-start = (s32[256]{0:T(256)S(1)}, s32[256]{0:T(256)}, u32[]{:S(2)}) copy-start(s32[256]{0:T(256)} %param.17) | copy-start | bytes 3076
  0.6 83.6 %copy-start.1 = (bf16[1,1,576,2048]{3,2,1,0:T(8,128)(2,1)S(1)}, bf16[1,1,576,2048]{3,2,1,0:T(8,128)(2,1)}, u32[]{:S(2)}) copy-start(bf16[1,1,576,2048]{3,2,1,0:T(8,128)(2,1)} %param.13) | copy-start | bytes 7077892
  0.7 83.6 %copy-start.7 = (bf16[1,1,576,16]{2,3,1,0:T(8,128)(2,1)S(1)}, bf16[1,1,576,16]{2,3,1,0:T(8,128)(2,1)}, u32[]{:S(2)}) copy-start(bf16[1,1,576,16]{2,3,1,0:T(8,128)(2,1)} %param.15) | copy-start | bytes 55300
  0.7 83.6 %copy-start.8 = (bf16[1,1,576,16]{2,3,1,0:T(8,128)(2,1)S(1)}, bf16[1,1,576,16]{2,3,1,0:T(8,128)(2,1)}, u32[]{:S(2)}) copy-start(bf16[1,1,576,16]{2,3,1,0:T(8,128)(2,1)} %param.16) | copy-start | bytes 55300
  0.7 83.6 %copy-start.9 = (s32[1,576]{1,0:T(1,128)S(1)}, s32[1,576]{1,0:T(1,128)}, u32[]{:S(2)}) copy-start(s32[1,576]{1,0:T(1,128)} %row_ref.1) | copy-start | bytes 6916
  0.7 83.6 %copy-start.10 = (s32[1,576]{1,0:T(1,128)S(1)}, s32[1,576]{1,0:T(1,128)}, u32[]{:S(2)}) copy-start(s32[1,576]{1,0:T(1,128)} %expert_ref.1) | copy-start | bytes 6916
  0.7 83.6 %copy-start.11 = (s32[1,64]{1,0:T(1,128)S(1)}, s32[1,64]{1,0:T(1,128)}, u32[]{:S(2)}) copy-start(s32[1,64]{1,0:T(1,128)} %count_ref.1) | copy-start | bytes 772
  0.7 83.6 %copy-start.12 = (s32[1,64]{1,0:T(1,128)S(1)}, s32[1,64]{1,0:T(1,128)}, u32[]{:S(2)}) copy-start(s32[1,64]{1,0:T(1,128)} %offset_ref.1) | copy-start | bytes 772
  84.6 2.8 %copy-start.6 = (bf16[2,4,48,2048]{3,2,1,0:T(8,128)(2,1)S(1)}, bf16[2,4,48,2048]{3,2,1,0:T(8,128)(2,1)}, u32[]{:S(2)}) copy-start(bf16[2,4,48,2048]{3,2,1,0:T(8,128)(2,1)} %get-tuple-element.155) | copy-start | bytes 4718596

commit v3 on v2

--- a/solution.py
+++ b/solution.py
@@ -151,18 +151,23 @@
     part_y,
     send,
     recv,
-    meta_send,
-    meta_recv,
+    land_own,
+    land_plane,
+    land_part,
+    land_z,
     grads,
     total_grad,
     place,
     late,
     wide_scales,
+    dir_out,
+    codes_out,
     load_sem,
+    store_sem,
     send_sem,
     recv_sem,
-    meta_ssem,
-    meta_rsem,
+    land_ssem,
+    land_rsem,
     grad_ssem,
     grad_rsem,
     core_sem,
@@ -170,6 +175,7 @@
     y_rsem,
     z_ssem,
     z_rsem,
+    ready,
 ):
     d = lax.axis_index("dp")
     e = lax.axis_index("expert")
@@ -198,15 +204,12 @@
 
     barrier = pltpu.get_barrier_semaphore()
 
-    def greet(i, carry):
+    for i in list(range(1, 8)) + list(range(8, 64, 8)):
         pl.semaphore_signal(barrier, inc=1, device_id=(d, peer(i)), device_id_type=MESH)
-        return carry
-
     for dx in range(1, 4):
         pl.semaphore_signal(
             barrier, inc=1, device_id=(lax.rem(d + dx, 4), e), device_id_type=MESH
         )
-    lax.fori_loop(1, 64, greet, 0)
 
     count = count_ref[...].astype(f32)
     offset = offset_ref[...].astype(f32)
@@ -243,10 +246,76 @@
                 [upper, lower], axis=1
             ).astype(bf16)
 
+    def remote(source, target, send_s, recv_s, to):
+        return pltpu.make_async_remote_copy(
+            src_ref=source,
+            dst_ref=target,
+            send_sem=send_s,
+            recv_sem=recv_s,
+            device_id=(d, to),
+            device_id_type=MESH,
+        )
+
+    def land_plane_copy(i):
+        to = peer(i)
+        return remote(
+            land_own.at[pl.ds(pl.multiple_of(lax.rem(to, 8) * 8, 8), 8)],
+            land_plane.at[i],
+            land_ssem.at[i],
+            land_rsem.at[i],
+            to,
+        )
+
+    def land_z_copy(dz):
+        to = lax.rem(z + dz, 8)
+        return remote(
+            land_part.at[pl.ds(to, 1)],
+            land_z.at[pl.ds(dz, 1)],
+            land_ssem.at[8 + dz],
+            land_rsem.at[8 + dz],
+            to * 8 + y * 2 + k,
+        )
+
+    urow, ocol = iota((64, 64), 0), iota((64, 64), 1)
+    mine = (((urow & 7) << 3) | (urow >> 3)) == ocol
+    count_col = pick(64, mine, count)
+    offset_col = pick(64, mine, offset)
+    lane = iota((64, slots), 1).astype(f32)
+    held = jnp.logical_and(lane >= offset_col, lane < offset_col + count_col)
+    rank = iota((1, slots), 1).astype(f32) - jnp.sum(
+        jnp.where(held, offset_col, 0.0), axis=0, keepdims=True
+    )
+    old_place = iota((256, slots), 0) == expert_ref[...]
+    mapped = dot(
+        jnp.broadcast_to(map_ref[...].astype(f32), (8, 256)).astype(bf16), old_place.astype(bf16)
+    )[0:1]
+    land = (mapped - 4.0 * jnp.floor(mapped * 0.25)) * float(share) + row_ref[...].astype(f32) + 1.0
+    held_land = jnp.where(held, land, 0.0).astype(bf16)
+    at_rank = (iota((128, slots), 0).astype(f32) == rank).astype(bf16)
+    targets = dot(held_land, at_rank, ((1,), (1,)))
+    slot, lane = iota((128, 384), 0), iota((128, 384), 1)
+    first = jnp.logical_and(slot < BASE, lane == e * BASE + slot)
+    later = jnp.logical_and(slot >= BASE, lane == 256 + slot - BASE)
+    keep = jnp.where(jnp.logical_or(first, later), 1.0, 0.0).astype(bf16)
+    tell = (iota((64, 384), 0) + 320 == iota((64, 384), 1)).astype(bf16)
+    heavy = jnp.broadcast_to((count > float(BASE)).astype(f32), (64, 64)).astype(bf16)
+    land_own[...] = dot(targets.astype(bf16), keep) + dot(heavy, tell)
+
     dequantize_half(0)
+    pl.semaphore_wait(barrier, 17)
+    for i in range(1, 8):
+        pl.semaphore_signal(ready, inc=1, device_id=(d, peer(i)), device_id_type=MESH)
+    for i in range(1, 8):
+        land_plane_copy(i).start()
     pack(0)
-
-    pl.semaphore_wait(barrier, 66)
+    for i in range(1, 8):
+        land_plane_copy(i).wait()
+    land_plane[0] = land_own[pl.ds(pl.multiple_of(lax.rem(e, 8) * 8, 8), 8), :]
+    land_part[...] = jnp.sum(land_plane[...], axis=0)
+    for dz in range(1, 8):
+        land_z_copy(dz).start()
+    land_z[pl.ds(0, 1), :] = land_part[pl.ds(z, 1), :]
+    pl.semaphore_wait(ready, 7)
 
     def grad_copy(dx):
         to = lax.rem(d + dx, 4)
@@ -263,35 +332,13 @@
         grad_ref.at[0, :, pl.ds(pl.multiple_of(d * share, 16), share), :], grads.at[0], grad_ssem.at[0]
     )
 
-    def meta_copy(i):
-        to = peer(i)
-        return pltpu.make_async_remote_copy(
-            src_ref=meta_send.at[pl.ds(to, 1)],
-            dst_ref=meta_recv.at[pl.ds(i, 1)],
-            send_sem=meta_ssem.at[i],
-            recv_sem=meta_rsem.at[i],
-            device_id=(d, to),
-            device_id_type=MESH,
-        )
-
     def main_copy(p, i):
         to = peer(i)
-        return pltpu.make_async_remote_copy(
-            src_ref=send.at[p, to],
-            dst_ref=recv.at[p, i],
-            send_sem=send_sem.at[p, i],
-            recv_sem=recv_sem.at[p, i],
-            device_id=(d, to),
-            device_id_type=MESH,
-        )
-
-    def start_meta(i, carry):
-        meta_copy(i).start()
-        return carry
-
-    def wait_meta(i, carry):
-        meta_copy(i).wait()
-        return carry
+        return remote(send.at[p, to], recv.at[p, e], send_sem.at[p, to], recv_sem.at[p, e], to)
+
+    def main_arrival(p, i):
+        to = peer(i)
+        return remote(send.at[p, to], recv.at[p, to], send_sem.at[p, to], recv_sem.at[p, to], to)
 
     def start_main(p):
         def start(i, carry):
@@ -302,7 +349,7 @@
 
     def wait_main(p):
         def wait(i, carry):
-            main_copy(p, i).wait()
+            main_arrival(p, i).wait()
             return carry
 
         return wait
@@ -312,7 +359,7 @@
     own_grad.start()
     lax.fori_loop(24, 64, start_main(0), 0)
     lax.fori_loop(1, 24, start_main(0), 0)
-    recv[0, 0] = send[0, e]
+    recv[0, e] = send[0, e]
 
     dequantize_half(1)
     row, col = iota((64 * EXTRA, 64), 0), iota((64 * EXTRA, 64), 1)
@@ -382,26 +429,6 @@
         y_copy(dy).start()
     lax.fori_loop(24, 48, start_main(1), 0)
 
-    orow, ocol = iota((64, 64), 0), iota((64, 64), 1)
-    count_col = pick(64, orow == ocol, count)
-    offset_col = pick(64, orow == ocol, offset)
-    lane = iota((64, slots), 1).astype(f32)
-    held = jnp.logical_and(lane >= offset_col, lane < offset_col + count_col)
-    rank = iota((1, slots), 1).astype(f32) - jnp.sum(
-        jnp.where(held, offset_col, 0.0), axis=0, keepdims=True
-    )
-    old_place = iota((256, slots), 0) == expert_ref[...]
-    mapped = dot(
-        jnp.broadcast_to(map_ref[...].astype(f32), (8, 256)).astype(bf16), old_place.astype(bf16)
-    )[0:1]
-    land = (mapped - 4.0 * jnp.floor(mapped * 0.25)) * float(share) + row_ref[...].astype(f32) + 1.0
-    held_land = jnp.where(held, land, 0.0).astype(bf16)
-    at_rank = (iota((128, slots), 0).astype(f32) == rank).astype(bf16)
-    targets = dot(held_land, at_rank, ((1,), (1,)))
-    shift = (iota((64, 128), 0) + 64 == iota((64, 128), 1)).astype(bf16)
-    counts = dot(jnp.broadcast_to(count, (64, 64)).astype(bf16), shift)
-    meta_send[...] = jnp.where(iota((64, 128), 1) < 16, targets, counts)
-
     for dy in range(1, 4):
         y_copy(dy).wait()
 
@@ -414,10 +441,8 @@
         z_copy(dz).start()
     lax.fori_loop(48, 64, start_main(1), 0)
     lax.fori_loop(1, 24, start_main(1), 0)
-    lax.fori_loop(1, 64, start_meta, 0)
-
-    recv[1, 0] = send[1, e]
-    meta_recv[pl.ds(0, 1), :] = meta_send[pl.ds(e, 1), :]
+
+    recv[1, e] = send[1, e]
 
     own_grad.wait()
     for dx in range(1, 4):
@@ -427,29 +452,24 @@
             grads[2, ex].astype(f32) + grads[3, ex].astype(f32)
         )
 
-    lax.fori_loop(1, 64, wait_meta, 0)
-    meta = meta_recv[...]
-
-    heavy = jnp.sum((meta > float(BASE)).astype(f32), axis=0, keepdims=True)
-    heavy = jnp.where(iota((1, 128), 1) >= 64, heavy, 0.0)
-    flag_ref[0] = jnp.max(heavy).astype(jnp.int32)
-
-    spread = (iota((64, 1024), 0) == (iota((64, 1024), 1) >> 4)).astype(bf16)
-    by_slot = dot(meta.astype(bf16), spread, ((0,), (0,)))[0:8]
+    for dz in range(1, 8):
+        land_z_copy(dz).wait()
+    landing = jnp.sum(land_z[...], axis=0, keepdims=True)
+    flag_ref[0] = jnp.max(landing[:, 256:] * (iota((1, 128), 1) >= 64).astype(f32)).astype(jnp.int32)
+    near, lane = iota((256, 1024), 0), iota((256, 1024), 1)
+    spread = jnp.logical_and((near >> 2) == (lane >> 4), (near & 3) == (lane & 3))
+    goal = dot(
+        jnp.broadcast_to(landing[:, :256], (8, 256)).astype(bf16),
+        jnp.where(spread, 1.0, 0.0).astype(bf16),
+    )[0:1]
     lane = iota((1, 1024), 1)
-    goal = jnp.sum(
-        jnp.where(iota((8, 1024), 0) == (lane & 3), by_slot, 0.0), axis=0, keepdims=True
-    )
     hit = iota((owned, 1024), 0).astype(f32) + 1.0 == goal
     for q in range(4):
         place[q * owned : (q + 1) * owned, :] = jnp.where(
             jnp.logical_and(hit, ((lane >> 2) & 3) == q), 1.0, 0.0
         ).astype(bf16)
-    late_goal = jnp.sum(meta, axis=0, keepdims=True)
-    late_lane = iota((owned, 128), 1)
     late_hit = jnp.logical_and(
-        iota((owned, 128), 0).astype(f32) + 1.0 == late_goal,
-        jnp.logical_and(late_lane >= BASE, late_lane < BASE + EXTRA),
+        iota((owned, 128), 0).astype(f32) + 1.0 == landing[:, 256:], iota((owned, 128), 1) < EXTRA
     )
     late_place = jnp.where(late_hit, 1.0, 0.0).astype(bf16)[:, :16]
 
@@ -459,7 +479,7 @@
     total = part_y[z].astype(f32)
     for dz in range(1, 8):
         total = total + extra_z[dz - 1].astype(f32)
-    late[BASE * 32 : (BASE + EXTRA) * 32, :] = total
+    late[: EXTRA * 32, :] = total
 
     def unpack(p):
         for c in range(2):
@@ -486,12 +506,12 @@
                 g = total_grad[ex, :, out]
                 m = beta_one * relay[at, :] + (1.0 - beta_one) * g
                 v = beta_two * relay[at_v, :] + (1.0 - beta_two) * g * g
-                dir_ref[ex, :, out] = m / (jnp.sqrt(v) + adam_eps)
+                dir_out[ex, :, out] = m / (jnp.sqrt(v) + adam_eps)
                 m_scale = (jnp.max(jnp.abs(m), axis=1, keepdims=True) + scale_eps).astype(bf16)
                 v_scale = (jnp.max(jnp.abs(v), axis=1, keepdims=True) + scale_eps).astype(bf16)
                 m_wide, v_wide = m_scale.astype(f32), v_scale.astype(f32)
-                codes_ref[0, ex, :, out] = (m * (1.0 / m_wide)).astype(bf16)
-                codes_ref[1, ex, :, out] = (v * (1.0 / v_wide)).astype(bf16)
+                codes_out[0, ex, :, out] = (m * (1.0 / m_wide)).astype(bf16)
+                codes_out[1, ex, :, out] = (v * (1.0 / v_wide)).astype(bf16)
                 m_scales = jnp.where(scale_lane == b, m_wide, m_scales)
                 v_scales = jnp.where(scale_lane == b, v_wide, v_scales)
             wide_scales[0, ex] = m_scales
@@ -500,19 +520,74 @@
 
         lax.fori_loop(0, 4, one, 0)
 
+    def stores(p):
+        copies = []
+        for h in range(2):
+            lanes = pl.ds(h * 1024 + p * 512, 512)
+            n = (p * 2 + h) * 2
+            copies.append(
+                pltpu.make_async_copy(
+                    dir_out.at[:, :, lanes], dir_ref.at[:, :, lanes], store_sem.at[n]
+                )
+            )
+            copies.append(
+                pltpu.make_async_copy(
+                    codes_out.at[:, :, :, lanes], codes_ref.at[:, :, :, lanes], store_sem.at[n + 1]
+                )
+            )
+        return copies
+
     wide_scales[...] = jnp.zeros_like(wide_scales)
-    lax.fori_loop(1, 64, wait_main(0), 0)
-    unpack(0)
-    update(0)
-    lax.fori_loop(1, 64, wait_main(1), 0)
-    unpack(1)
-    update(1)
+    for p in range(2):
+        lax.fori_loop(1, 64, wait_main(p), 0)
+        unpack(p)
+        update(p)
+        for copy in stores(p):
+            copy.start()
     turn = (iota((share, share), 0) == iota((share, share), 1)).astype(bf16)
     for part in range(2):
         for ex in range(4):
             scales_ref[part, ex] = dot(
                 wide_scales[part, ex].astype(bf16), turn, ((0,), (0,))
             ).astype(bf16)
+    for p in range(2):
+        for copy in stores(p):
+            copy.wait()
+
+
+def hand_on_kernel(dir_ref, codes_ref, scales_ref, dir_to, codes_to, scales_to, dirs, codes, scales, sem):
+    pieces = [(scales_ref, scales, scales_to)]
+    for ex in range(4):
+        pieces.append((dir_ref.at[ex], dirs.at[ex], dir_to.at[ex]))
+        for part in range(2):
+            pieces.append((codes_ref.at[part, ex], codes.at[part, ex], codes_to.at[part, ex]))
+    loads = [
+        pltpu.make_async_copy(source, held, sem.at[0, n]) for n, (source, held, _) in enumerate(pieces)
+    ]
+    stores = [
+        pltpu.make_async_copy(held, target, sem.at[1, n]) for n, (_, held, target) in enumerate(pieces)
+    ]
+    for copy in loads:
+        copy.start()
+    for first, second in zip(loads, stores):
+        first.wait()
+        second.start()
+    for copy in stores:
+        copy.wait()
+
+
+def hand_on(*results):
+    return tuple(
+        pl.pallas_call(
+            hand_on_kernel,
+            out_shape=tuple(jax.ShapeDtypeStruct(r.shape, r.dtype) for r in results),
+            in_specs=[pl.BlockSpec(memory_space=pl.ANY)] * 3,
+            out_specs=(pl.BlockSpec(memory_space=pl.ANY),) * 3,
+            scratch_shapes=[pltpu.VMEM(r.shape, r.dtype) for r in results]
+            + [pltpu.SemaphoreType.DMA((2, 13))],
+            name="hand_on",
+        )(*results)
+    )
 
 
 def exchange(grad_parts, m_codes, v_codes, m_scale, v_scale, expert_map, slot_expert, slot_row, count, offset):
@@ -531,7 +606,7 @@
             jax.ShapeDtypeStruct((1,), jnp.int32),
         ),
         in_specs=[hbm] * 3 + [vmem] * 7,
-        out_specs=(vmem,) * 3 + (pl.BlockSpec(memory_space=pltpu.SMEM),),
+        out_specs=(hbm, hbm, vmem, pl.BlockSpec(memory_space=pltpu.SMEM)),
         scratch_shapes=[
             pltpu.VMEM((slots, 2 * width), bf16),
             pltpu.VMEM((slots, 2 * width), bf16),
@@ -544,18 +619,23 @@
             pltpu.VMEM((8, chunk, 128), bf16),
             pltpu.VMEM((2, 64, 16, 512), bf16),
             pltpu.VMEM((2, 64, 16, 512), bf16),
-            pltpu.VMEM((64, 128), f32),
-            pltpu.VMEM((64, 128), f32),
+            pltpu.VMEM((64, 384), f32),
+            pltpu.VMEM((8, 8, 384), f32),
+            pltpu.VMEM((8, 384), f32),
+            pltpu.VMEM((8, 384), f32),
             pltpu.VMEM((4, 4, share, width), bf16),
             pltpu.VMEM((4, share, width), f32),
             pltpu.VMEM((4 * owned, 1024), bf16),
             pltpu.VMEM((16 * 32, 128), f32),
             pltpu.VMEM((2, 4, share, 16), f32),
+            pltpu.VMEM((4, share, width), f32),
+            pltpu.VMEM((2, 4, share, width), bf16),
+            pltpu.SemaphoreType.DMA((8,)),
             pltpu.SemaphoreType.DMA((8,)),
             pltpu.SemaphoreType.DMA((2, 64)),
             pltpu.SemaphoreType.DMA((2, 64)),
-            pltpu.SemaphoreType.DMA((64,)),
-            pltpu.SemaphoreType.DMA((64,)),
+            pltpu.SemaphoreType.DMA((16,)),
+            pltpu.SemaphoreType.DMA((16,)),
             pltpu.SemaphoreType.DMA((4,)),
             pltpu.SemaphoreType.DMA((4,)),
             pltpu.SemaphoreType.DMA((2,)),
@@ -563,6 +643,7 @@
             pltpu.SemaphoreType.DMA((3,)),
             pltpu.SemaphoreType.DMA((7,)),
             pltpu.SemaphoreType.DMA((7,)),
+            pltpu.SemaphoreType.REGULAR,
         ],
         compiler_params=pltpu.CompilerParams(
             collective_id=0, has_side_effects=True, vmem_limit_bytes=VMEM_MIB * 2**20
@@ -580,16 +661,20 @@
         count,
         offset,
     )
-    return direction, codes, jnp.swapaxes(scales, 2, 3), heavy
+    return direction, codes, scales, heavy
 
 
 def per_device(*args):
     direction, codes, scales, heavy = exchange(*args)
-    return lax.cond(
-        heavy[0] < 2,
-        lambda: (direction, codes, scales),
-        lambda: padded_exchange(*args),
-    )
+
+    def padded():
+        direction, codes, scales = padded_exchange(*args)
+        return direction, codes, jnp.swapaxes(scales, 2, 3)
+
+    direction, codes, scales = lax.cond(
+        heavy[0] < 2, lambda: hand_on(direction, codes, scales), padded
+    )
+    return direction, codes, jnp.swapaxes(scales, 2, 3)
 
 
 def solution(mesh):

time: 89.3 us -> 84.7 us (0.948)
  local copies, waits for them, and re-layouts: 4.61 us -> 0.03 us
    unnamed x21 -> x16, local copies, waits for them, and re-layouts: 4.61 us -> 0.03 us
    pallas_call x1, Pallas kernels: 82.9 us -> 79.7 us  [exchange(): pl.pallas_call(resume_kernel, out_shape=(jax.ShapeDtypeStruct((4, share,...]
    pallas_call x0 -> x1, Pallas kernels: none -> 2.94 us  [hand_on(): pl.pallas_call(hand_on_kernel, out_shape=tuple((jax.ShapeDtypeStruct(r.sh...]
where the time goes in v3:
time: 84.7 us; the launch traced here: 84.6 us
  Pallas kernels  82.7 us (98%)
  between operations  1.6 us (2%)
    pallas_call x1, Pallas kernels, exchange(): pl.pallas_call(resume_kernel, out_shape=(jax.ShapeDtypeStruct((4, share,...  79.7 us
    pallas_call x1, Pallas kernels, hand_on(): pl.pallas_call(hand_on_kernel, out_shape=tuple((jax.ShapeDtypeStruct(r.sh...  2.94 us

profile of v3, /device:TPU:1, one launch (start us, length us, event | category | flops | bytes accessed | tf_op | source)
XLA Modules:
  0.0 84.6 jit_solution(1904113502309331624)
XLA Ops:
  0.6 0.0 copy-start
  0.6 0.0 copy-start.1
  0.7 0.0 copy-start.6
  0.7 0.0 copy-start.7
  0.7 0.0 copy-start.8
  0.7 0.0 copy-start.9
  0.7 0.0 copy-start.10
  0.7 0.0 copy-start.11
  0.7 79.7 %resume.1 = (f32[4,48,2048]{2,1,0:T(8,128)}, bf16[2,4,48,2048]{3,2,1,0:T(8,128)(2,1)}, bf16[2,4,16,48]{3,2,1,0:T(8,128)(2,1)S(1)}, s32[1]{0:T(128)}) custom-call(bf16[1,4,192,2048]{3,2,1,0:T(8,128)(2,1)} %grad_ref.1, bf16[576,2048]{1,0:T(8,128)(2,1)} %bitcast.71, bf16[576,2048]{1,0:T(8,128)(2,1)} %bitcast.73, bf16[16,576]{1,0:T(8,128)(2,1)} %bitcast.86, ...), custom_call_target="tpu_custom_call" | custom-call | tf_op jit(solution)/shard_map/resume/pallas_call | solution.py:600
  81.1 0.0 copy-done
  81.1 0.0 copy-done.1
  81.1 0.0 copy-done.6
  81.1 0.0 copy-done.7
  81.1 0.0 copy-done.8
  81.1 0.0 copy-done.9
  81.1 0.0 copy-done.10
  81.2 0.0 copy-done.11
  81.2 3.2 %conditional.1 = ((f32[4,48,2048]{2,1,0:T(8,128)}, bf16[2,4,48,2048]{3,2,1,0:T(8,128)(2,1)}, bf16[2,4,16,48]{3,2,1,0:T(8,128)(2,1)})) conditional(s32[]{:T(128)} %bitcast.24, (s32[1,64]{1,0:T(1,128)S(1)}, s32[1,576]{1,0:T(1,128)S(1)}, s32[256]{0:T(256)S(1)}, s32[1,576]{1,0:T(1,128)S(1)}, s32[1,64]{1,0:T(1,128)S(1)}, ...), branch_computations={%region_0.6_spmd, %region_6.7_spmd} | conditional | flops 18910400 | bytes 215458336 | solution.py:674
  81.4 2.9 %hand_on.1 = (f32[4,48,2048]{2,1,0:T(8,128)}, bf16[2,4,48,2048]{3,2,1,0:T(8,128)(2,1)}, bf16[2,4,16,48]{3,2,1,0:T(8,128)(2,1)}) custom-call(f32[4,48,2048]{2,1,0:T(8,128)} %get-tuple-element.36.dir_ref, bf16[2,4,48,2048]{3,2,1,0:T(8,128)(2,1)} %get-tuple-element.37.codes_ref, bf16[2,4,16,48]{3,2,1,0:T(8,128)(2,1)S(1)} %get-tuple-element.38.scales_ref), custom_call_target="tpu_custom_call" | custom-call | tf_op jit(solution)/shard_map/cond/branch_1_fun/hand_on/pallas_call | solution.py:581
Async XLA Ops:
  0.6 80.5 %copy-start = (s32[256]{0:T(256)S(1)}, s32[256]{0:T(256)}, u32[]{:S(2)}) copy-start(s32[256]{0:T(256)} %param.17) | copy-start | bytes 3076
  0.6 80.5 %copy-start.1 = (bf16[1,1,576,2048]{3,2,1,0:T(8,128)(2,1)S(1)}, bf16[1,1,576,2048]{3,2,1,0:T(8,128)(2,1)}, u32[]{:S(2)}) copy-start(bf16[1,1,576,2048]{3,2,1,0:T(8,128)(2,1)} %param.13) | copy-start | bytes 7077892
  0.7 80.5 %copy-start.6 = (bf16[1,1,576,16]{2,3,1,0:T(8,128)(2,1)S(1)}, bf16[1,1,576,16]{2,3,1,0:T(8,128)(2,1)}, u32[]{:S(2)}) copy-start(bf16[1,1,576,16]{2,3,1,0:T(8,128)(2,1)} %param.15) | copy-start | bytes 55300
  0.7 80.5 %copy-start.7 = (bf16[1,1,576,16]{2,3,1,0:T(8,128)(2,1)S(1)}, bf16[1,1,576,16]{2,3,1,0:T(8,128)(2,1)}, u32[]{:S(2)}) copy-start(bf16[1,1,576,16]{2,3,1,0:T(8,128)(2,1)} %param.16) | copy-start | bytes 55300
  0.7 80.5 %copy-start.8 = (s32[1,576]{1,0:T(1,128)S(1)}, s32[1,576]{1,0:T(1,128)}, u32[]{:S(2)}) copy-start(s32[1,576]{1,0:T(1,128)} %row_ref.1) | copy-start | bytes 6916
  0.7 80.5 %copy-start.9 = (s32[1,576]{1,0:T(1,128)S(1)}, s32[1,576]{1,0:T(1,128)}, u32[]{:S(2)}) copy-start(s32[1,576]{1,0:T(1,128)} %expert_ref.1) | copy-start | bytes 6916
  0.7 80.5 %copy-start.10 = (s32[1,64]{1,0:T(1,128)S(1)}, s32[1,64]{1,0:T(1,128)}, u32[]{:S(2)}) copy-start(s32[1,64]{1,0:T(1,128)} %count_ref.1) | copy-start | bytes 772
  0.7 80.5 %copy-start.11 = (s32[1,64]{1,0:T(1,128)S(1)}, s32[1,64]{1,0:T(1,128)}, u32[]{:S(2)}) copy-start(s32[1,64]{1,0:T(1,128)} %offset_ref.1) | copy-start | bytes 772

commit v4 on v3

--- a/solution.py
+++ b/solution.py
@@ -160,10 +160,7 @@
     place,
     late,
     wide_scales,
-    dir_out,
-    codes_out,
     load_sem,
-    store_sem,
     send_sem,
     recv_sem,
     land_ssem,
@@ -308,13 +305,6 @@
     for i in range(1, 8):
         land_plane_copy(i).start()
     pack(0)
-    for i in range(1, 8):
-        land_plane_copy(i).wait()
-    land_plane[0] = land_own[pl.ds(pl.multiple_of(lax.rem(e, 8) * 8, 8), 8), :]
-    land_part[...] = jnp.sum(land_plane[...], axis=0)
-    for dz in range(1, 8):
-        land_z_copy(dz).start()
-    land_z[pl.ds(0, 1), :] = land_part[pl.ds(z, 1), :]
     pl.semaphore_wait(ready, 7)
 
     def grad_copy(dx):
@@ -332,33 +322,41 @@
         grad_ref.at[0, :, pl.ds(pl.multiple_of(d * share, 16), share), :], grads.at[0], grad_ssem.at[0]
     )
 
-    def main_copy(p, i):
-        to = peer(i)
-        return remote(send.at[p, to], recv.at[p, e], send_sem.at[p, to], recv_sem.at[p, e], to)
-
-    def main_arrival(p, i):
-        to = peer(i)
-        return remote(send.at[p, to], recv.at[p, to], send_sem.at[p, to], recv_sem.at[p, to], to)
-
-    def start_main(p):
-        def start(i, carry):
-            main_copy(p, i).start()
+    columns_of = [lax.rem(y + j // 2, 4) * 2 + lax.rem(k + j % 2, 2) for j in range(8)]
+
+    def start_main(p, low, high):
+        def plane(dz, carry):
+            base = lax.rem(z + dz, 8) * 8
+            for j in range(8):
+                to = base + columns_of[j]
+                remote(send.at[p, to], recv.at[p, e], send_sem.at[p], recv_sem.at[p], to).start()
             return carry
 
-        return start
+        lax.fori_loop(low, high, plane, 0)
+
+    def start_own_plane(p):
+        for j in range(1, 8):
+            to = z * 8 + columns_of[j]
+            remote(send.at[p, to], recv.at[p, e], send_sem.at[p], recv_sem.at[p], to).start()
 
     def wait_main(p):
-        def wait(i, carry):
-            main_arrival(p, i).wait()
-            return carry
-
-        return wait
+        all_others = pl.ds(0, 63)
+        remote(
+            send.at[p, all_others], recv.at[p, all_others], send_sem.at[p], recv_sem.at[p], peer(1)
+        ).wait()
 
     for dx in range(1, 4):
         grad_copy(dx).start()
     own_grad.start()
-    lax.fori_loop(24, 64, start_main(0), 0)
-    lax.fori_loop(1, 24, start_main(0), 0)
+    start_main(0, 1, 8)
+    start_own_plane(0)
+    for i in range(1, 8):
+        land_plane_copy(i).wait()
+    land_plane[0] = land_own[pl.ds(pl.multiple_of(lax.rem(e, 8) * 8, 8), 8), :]
+    land_part[...] = jnp.sum(land_plane[...], axis=0)
+    for dz in range(1, 8):
+        land_z_copy(dz).start()
+    land_z[pl.ds(0, 1), :] = land_part[pl.ds(z, 1), :]
     recv[0, e] = send[0, e]
 
     dequantize_half(1)
@@ -427,7 +425,7 @@
 
     for dy in range(1, 4):
         y_copy(dy).start()
-    lax.fori_loop(24, 48, start_main(1), 0)
+    start_main(1, 3, 6)
 
     for dy in range(1, 4):
         y_copy(dy).wait()
@@ -439,8 +437,9 @@
     lax.fori_loop(0, 8, add_y, 0)
     for dz in range(1, 8):
         z_copy(dz).start()
-    lax.fori_loop(48, 64, start_main(1), 0)
-    lax.fori_loop(1, 24, start_main(1), 0)
+    start_main(1, 6, 8)
+    start_main(1, 1, 3)
+    start_own_plane(1)
 
     recv[1, e] = send[1, e]
 
@@ -506,12 +505,12 @@
                 g = total_grad[ex, :, out]
                 m = beta_one * relay[at, :] + (1.0 - beta_one) * g
                 v = beta_two * relay[at_v, :] + (1.0 - beta_two) * g * g
-                dir_out[ex, :, out] = m / (jnp.sqrt(v) + adam_eps)
+                dir_ref[ex, :, out] = m / (jnp.sqrt(v) + adam_eps)
                 m_scale = (jnp.max(jnp.abs(m), axis=1, keepdims=True) + scale_eps).astype(bf16)
                 v_scale = (jnp.max(jnp.abs(v), axis=1, keepdims=True) + scale_eps).astype(bf16)
                 m_wide, v_wide = m_scale.astype(f32), v_scale.astype(f32)
-                codes_out[0, ex, :, out] = (m * (1.0 / m_wide)).astype(bf16)
-                codes_out[1, ex, :, out] = (v * (1.0 / v_wide)).astype(bf16)
+                codes_ref[0, ex, :, out] = (m * (1.0 / m_wide)).astype(bf16)
+                codes_ref[1, ex, :, out] = (v * (1.0 / v_wide)).astype(bf16)
                 m_scales = jnp.where(scale_lane == b, m_wide, m_scales)
                 v_scales = jnp.where(scale_lane == b, v_wide, v_scales)
             wide_scales[0, ex] = m_scales
@@ -520,59 +519,32 @@
 
         lax.fori_loop(0, 4, one, 0)
 
-    def stores(p):
-        copies = []
-        for h in range(2):
-            lanes = pl.ds(h * 1024 + p * 512, 512)
-            n = (p * 2 + h) * 2
-            copies.append(
-                pltpu.make_async_copy(
-                    dir_out.at[:, :, lanes], dir_ref.at[:, :, lanes], store_sem.at[n]
-                )
-            )
-            copies.append(
-                pltpu.make_async_copy(
-                    codes_out.at[:, :, :, lanes], codes_ref.at[:, :, :, lanes], store_sem.at[n + 1]
-                )
-            )
-        return copies
-
     wide_scales[...] = jnp.zeros_like(wide_scales)
     for p in range(2):
-        lax.fori_loop(1, 64, wait_main(p), 0)
+        wait_main(p)
         unpack(p)
         update(p)
-        for copy in stores(p):
-            copy.start()
     turn = (iota((share, share), 0) == iota((share, share), 1)).astype(bf16)
     for part in range(2):
         for ex in range(4):
             scales_ref[part, ex] = dot(
                 wide_scales[part, ex].astype(bf16), turn, ((0,), (0,))
             ).astype(bf16)
-    for p in range(2):
-        for copy in stores(p):
-            copy.wait()
-
-
-def hand_on_kernel(dir_ref, codes_ref, scales_ref, dir_to, codes_to, scales_to, dirs, codes, scales, sem):
-    pieces = [(scales_ref, scales, scales_to)]
+
+
+def hand_on_kernel(dir_ref, codes_ref, scales_ref, dir_to, codes_to, scales_to, sem):
+    copies = [pltpu.make_async_copy(scales_ref, scales_to, sem.at[12])]
     for ex in range(4):
-        pieces.append((dir_ref.at[ex], dirs.at[ex], dir_to.at[ex]))
+        copies.append(pltpu.make_async_copy(dir_ref.at[ex], dir_to.at[ex], sem.at[ex]))
         for part in range(2):
-            pieces.append((codes_ref.at[part, ex], codes.at[part, ex], codes_to.at[part, ex]))
-    loads = [
-        pltpu.make_async_copy(source, held, sem.at[0, n]) for n, (source, held, _) in enumerate(pieces)
-    ]
-    stores = [
-        pltpu.make_async_copy(held, target, sem.at[1, n]) for n, (_, held, target) in enumerate(pieces)
-    ]
-    for copy in loads:
+            copies.append(
+                pltpu.make_async_copy(
+                    codes_ref.at[part, ex], codes_to.at[part, ex], sem.at[4 + part * 4 + ex]
+                )
+            )
+    for copy in copies:
         copy.start()
-    for first, second in zip(loads, stores):
-        first.wait()
-        second.start()
-    for copy in stores:
+    for copy in copies:
         copy.wait()
 
 
@@ -581,12 +553,12 @@
         pl.pallas_call(
             hand_on_kernel,
             out_shape=tuple(jax.ShapeDtypeStruct(r.shape, r.dtype) for r in results),
-            in_specs=[pl.BlockSpec(memory_space=pl.ANY)] * 3,
+            in_specs=[pl.BlockSpec(memory_space=pltpu.VMEM)] * 3,
             out_specs=(pl.BlockSpec(memory_space=pl.ANY),) * 3,
-            scratch_shapes=[pltpu.VMEM(r.shape, r.dtype) for r in results]
-            + [pltpu.SemaphoreType.DMA((2, 13))],
+            scratch_shapes=[pltpu.SemaphoreType.DMA((13,))],
+            compiler_params=pltpu.CompilerParams(vmem_limit_bytes=8 * 2**20),
             name="hand_on",
-        )(*results)
+        )(*[pltpu.with_memory_space_constraint(r, pltpu.VMEM) for r in results])
     )
 
 
@@ -600,13 +572,13 @@
     direction, codes, scales, heavy = pl.pallas_call(
         resume_kernel,
         out_shape=(
-            jax.ShapeDtypeStruct((4, share, width), f32),
-            jax.ShapeDtypeStruct((2, 4, share, width), bf16),
-            jax.ShapeDtypeStruct((2, 4, blocks, share), bf16),
+            pltpu.VMEM((4, share, width), f32),
+            pltpu.VMEM((2, 4, share, width), bf16),
+            pltpu.VMEM((2, 4, blocks, share), bf16),
             jax.ShapeDtypeStruct((1,), jnp.int32),
         ),
         in_specs=[hbm] * 3 + [vmem] * 7,
-        out_specs=(hbm, hbm, vmem, pl.BlockSpec(memory_space=pltpu.SMEM)),
+        out_specs=(vmem, vmem, vmem, pl.BlockSpec(memory_space=pltpu.SMEM)),
         scratch_shapes=[
             pltpu.VMEM((slots, 2 * width), bf16),
             pltpu.VMEM((slots, 2 * width), bf16),
@@ -628,12 +600,9 @@
             pltpu.VMEM((4 * owned, 1024), bf16),
             pltpu.VMEM((16 * 32, 128), f32),
             pltpu.VMEM((2, 4, share, 16), f32),
-            pltpu.VMEM((4, share, width), f32),
-            pltpu.VMEM((2, 4, share, width), bf16),
             pltpu.SemaphoreType.DMA((8,)),
-            pltpu.SemaphoreType.DMA((8,)),
-            pltpu.SemaphoreType.DMA((2, 64)),
-            pltpu.SemaphoreType.DMA((2, 64)),
+            pltpu.SemaphoreType.DMA((2,)),
+            pltpu.SemaphoreType.DMA((2,)),
             pltpu.SemaphoreType.DMA((16,)),
             pltpu.SemaphoreType.DMA((16,)),
             pltpu.SemaphoreType.DMA((4,)),

time: 84.7 us -> 74.1 us (0.87)
  Pallas kernels: 82.7 us -> 72 us
    pallas_call x1, Pallas kernels: 79.7 us -> 70.3 us  [exchange(): pl.pallas_call(resume_kernel, out_shape=(pltpu.VMEM((4, share, width), f3...]
    pallas_call x1, Pallas kernels: 2.94 us -> 1.77 us  [hand_on(): pl.pallas_call(hand_on_kernel, out_shape=tuple((jax.ShapeDtypeStruct(r.sh...]
where the time goes in v4:
time: 74.1 us; the launch traced here: 73.9 us
  Pallas kernels  72 us (97%)
  between operations  1.56 us (2%)
    pallas_call x1, Pallas kernels, exchange(): pl.pallas_call(resume_kernel, out_shape=(pltpu.VMEM((4, share, width), f3...  70.3 us
    pallas_call x1, Pallas kernels, hand_on(): pl.pallas_call(hand_on_kernel, out_shape=tuple((jax.ShapeDtypeStruct(r.sh...  1.77 us

profile of v4, /device:TPU:1, one launch (start us, length us, event | category | flops | bytes accessed | tf_op | source)
XLA Modules:
  0.0 73.9 jit_solution(5207195042871643328)
XLA Ops:
  0.6 0.0 copy-start
  0.6 0.0 copy-start.7
  0.7 0.0 copy-start.8
  0.7 0.0 copy-start.9
  0.7 0.0 copy-start.10
  0.7 0.0 copy-start.11
  0.7 0.0 copy-start.12
  0.7 70.3 %resume.1 = (f32[4,48,2048]{2,1,0:T(8,128)S(1)}, bf16[2,4,48,2048]{3,2,1,0:T(8,128)(2,1)S(1)}, bf16[2,4,16,48]{3,2,1,0:T(8,128)(2,1)S(1)}, s32[1]{0:T(128)}) custom-call(bf16[1,4,192,2048]{3,2,1,0:T(8,128)(2,1)} %grad_ref.1, bf16[576,2048]{1,0:T(8,128)(2,1)} %bitcast.71, bf16[576,2048]{1,0:T(8,128)(2,1)} %bitcast.73, bf16[16,576]{1,0:T(8,128)(2,1)} %bitcast.86, ...), custom_call_target="tpu_custom_call" | custom-call | tf_op jit(solution)/shard_map/resume/pallas_call | solution.py:572
  71.6 0.0 copy-done
  71.6 0.0 copy-done.7
  71.6 0.0 copy-done.8
  71.6 0.0 copy-done.9
  71.6 0.0 copy-done.10
  71.6 0.0 copy-done.11
  71.6 0.0 copy-done.12
  71.7 2.1 %conditional.1 = ((f32[4,48,2048]{2,1,0:T(8,128)}, bf16[2,4,48,2048]{3,2,1,0:T(8,128)(2,1)}, bf16[2,4,16,48]{3,2,1,0:T(8,128)(2,1)})) conditional(s32[]{:T(128)} %bitcast.24, (s32[1,64]{1,0:T(1,128)S(1)}, s32[1,576]{1,0:T(1,128)S(1)}, s32[256]{0:T(256)S(1)}, s32[1,576]{1,0:T(1,128)S(1)}, s32[1,64]{1,0:T(1,128)S(1)}, ...), branch_computations={%region_0.6_spmd, %region_6.7_spmd} | conditional | flops 18910400 | bytes 237478496 | solution.py:643
  71.9 1.8 %hand_on.1 = (f32[4,48,2048]{2,1,0:T(8,128)}, bf16[2,4,48,2048]{3,2,1,0:T(8,128)(2,1)}, bf16[2,4,16,48]{3,2,1,0:T(8,128)(2,1)}) custom-call(f32[4,48,2048]{2,1,0:T(8,128)S(1)} %get-tuple-element.36.dir_ref, bf16[2,4,48,2048]{3,2,1,0:T(8,128)(2,1)S(1)} %get-tuple-element.37.codes_ref, bf16[2,4,16,48]{3,2,1,0:T(8,128)(2,1)S(1)} %get-tuple-element.38.scales_ref), custom_call_target="tpu_custom_call" | custom-call | tf_op jit(solution)/shard_map/cond/branch_1_fun/hand_on/pallas_call | solution.py:553
Async XLA Ops:
  0.6 71.0 %copy-start = (s32[256]{0:T(256)S(1)}, s32[256]{0:T(256)}, u32[]{:S(2)}) copy-start(s32[256]{0:T(256)} %param.17) | copy-start | bytes 3076
  0.6 71.0 %copy-start.7 = (bf16[1,1,576,16]{2,3,1,0:T(8,128)(2,1)S(1)}, bf16[1,1,576,16]{2,3,1,0:T(8,128)(2,1)}, u32[]{:S(2)}) copy-start(bf16[1,1,576,16]{2,3,1,0:T(8,128)(2,1)} %param.15) | copy-start | bytes 55300
  0.7 71.0 %copy-start.8 = (bf16[1,1,576,16]{2,3,1,0:T(8,128)(2,1)S(1)}, bf16[1,1,576,16]{2,3,1,0:T(8,128)(2,1)}, u32[]{:S(2)}) copy-start(bf16[1,1,576,16]{2,3,1,0:T(8,128)(2,1)} %param.16) | copy-start | bytes 55300
  0.7 71.0 %copy-start.9 = (s32[1,576]{1,0:T(1,128)S(1)}, s32[1,576]{1,0:T(1,128)}, u32[]{:S(2)}) copy-start(s32[1,576]{1,0:T(1,128)} %row_ref.1) | copy-start | bytes 6916
  0.7 71.0 %copy-start.10 = (s32[1,576]{1,0:T(1,128)S(1)}, s32[1,576]{1,0:T(1,128)}, u32[]{:S(2)}) copy-start(s32[1,576]{1,0:T(1,128)} %expert_ref.1) | copy-start | bytes 6916
  0.7 71.0 %copy-start.11 = (s32[1,64]{1,0:T(1,128)S(1)}, s32[1,64]{1,0:T(1,128)}, u32[]{:S(2)}) copy-start(s32[1,64]{1,0:T(1,128)} %count_ref.1) | copy-start | bytes 772
  0.7 71.0 %copy-start.12 = (s32[1,64]{1,0:T(1,128)S(1)}, s32[1,64]{1,0:T(1,128)}, u32[]{:S(2)}) copy-start(s32[1,64]{1,0:T(1,128)} %offset_ref.1) | copy-start | bytes 772

commit v5 on v4

--- a/solution.py
+++ b/solution.py
@@ -480,6 +480,13 @@
         total = total + extra_z[dz - 1].astype(f32)
     late[: EXTRA * 32, :] = total
 
+    def unpack_late(p):
+        for q in range(4):
+            for i in range(4):
+                block = q * 8 + p * 4 + i
+                rest = late[pl.ds(block, 16, stride=32), :].astype(bf16)
+                relay[block * owned : (block + 1) * owned, :] = dot(late_place, rest)
+
     def unpack(p):
         for c in range(2):
             arrived = dot(
@@ -487,11 +494,11 @@
             )
             for q in range(4):
                 for b in range(2):
-                    block = p * 4 + c * 2 + b
-                    rest = late[pl.ds(q * 8 + block, 16, stride=32), :].astype(bf16)
-                    relay[(q * 8 + block) * owned : (q * 8 + block + 1) * owned, :] = arrived[
+                    block = q * 8 + p * 4 + c * 2 + b
+                    rows = slice(block * owned, (block + 1) * owned)
+                    relay[rows, :] = relay[rows, :] + arrived[
                         q * owned : (q + 1) * owned, b * 128 : (b + 1) * 128
-                    ] + dot(late_place, rest)
+                    ]
 
     def update(p):
         def one(ex, carry):
@@ -521,6 +528,7 @@
 
     wide_scales[...] = jnp.zeros_like(wide_scales)
     for p in range(2):
+        unpack_late(p)
         wait_main(p)
         unpack(p)
         update(p)

time: 74.1 us -> 73.9 us (level)
  no operation moved by 1% of the time
where the time goes in v5:
time: 73.9 us; the launch traced here: 73.7 us
  Pallas kernels  71.8 us (97%)
  between operations  1.56 us (2%)
    pallas_call x1, Pallas kernels, exchange(): pl.pallas_call(resume_kernel, out_shape=(pltpu.VMEM((4, share, width), f3...  70.1 us
    pallas_call x1, Pallas kernels, hand_on(): pl.pallas_call(hand_on_kernel, out_shape=tuple((jax.ShapeDtypeStruct(r.sh...  1.77 us

profile of v5, /device:TPU:1, one launch (start us, length us, event | category | flops | bytes accessed | tf_op | source)
XLA Modules:
  0.0 73.7 jit_solution(10911118951193554866)
XLA Ops:
  0.6 0.0 copy-start
  0.6 0.0 copy-start.7
  0.7 0.0 copy-start.8
  0.7 0.0 copy-start.9
  0.7 0.0 copy-start.10
  0.7 0.0 copy-start.11
  0.7 0.0 copy-start.12
  0.7 70.1 %resume.1 = (f32[4,48,2048]{2,1,0:T(8,128)S(1)}, bf16[2,4,48,2048]{3,2,1,0:T(8,128)(2,1)S(1)}, bf16[2,4,16,48]{3,2,1,0:T(8,128)(2,1)S(1)}, s32[1]{0:T(128)}) custom-call(bf16[1,4,192,2048]{3,2,1,0:T(8,128)(2,1)} %grad_ref.1, bf16[576,2048]{1,0:T(8,128)(2,1)} %bitcast.71, bf16[576,2048]{1,0:T(8,128)(2,1)} %bitcast.73, bf16[16,576]{1,0:T(8,128)(2,1)} %bitcast.86, ...), custom_call_target="tpu_custom_call" | custom-call | tf_op jit(solution)/shard_map/resume/pallas_call | solution.py:580
  71.4 0.0 copy-done
  71.4 0.0 copy-done.7
  71.4 0.0 copy-done.8
  71.4 0.0 copy-done.9
  71.4 0.0 copy-done.10
  71.4 0.0 copy-done.11
  71.4 0.0 copy-done.12
  71.5 2.1 %conditional.1 = ((f32[4,48,2048]{2,1,0:T(8,128)}, bf16[2,4,48,2048]{3,2,1,0:T(8,128)(2,1)}, bf16[2,4,16,48]{3,2,1,0:T(8,128)(2,1)})) conditional(s32[]{:T(128)} %bitcast.24, (s32[1,64]{1,0:T(1,128)S(1)}, s32[1,576]{1,0:T(1,128)S(1)}, s32[256]{0:T(256)S(1)}, s32[1,576]{1,0:T(1,128)S(1)}, s32[1,64]{1,0:T(1,128)S(1)}, ...), branch_computations={%region_0.6_spmd, %region_6.7_spmd} | conditional | flops 18910400 | bytes 237478496 | solution.py:651
  71.7 1.8 %hand_on.1 = (f32[4,48,2048]{2,1,0:T(8,128)}, bf16[2,4,48,2048]{3,2,1,0:T(8,128)(2,1)}, bf16[2,4,16,48]{3,2,1,0:T(8,128)(2,1)}) custom-call(f32[4,48,2048]{2,1,0:T(8,128)S(1)} %get-tuple-element.36.dir_ref, bf16[2,4,48,2048]{3,2,1,0:T(8,128)(2,1)S(1)} %get-tuple-element.37.codes_ref, bf16[2,4,16,48]{3,2,1,0:T(8,128)(2,1)S(1)} %get-tuple-element.38.scales_ref), custom_call_target="tpu_custom_call" | custom-call | tf_op jit(solution)/shard_map/cond/branch_1_fun/hand_on/pallas_call | solution.py:561
Async XLA Ops:
  0.6 70.8 %copy-start = (s32[256]{0:T(256)S(1)}, s32[256]{0:T(256)}, u32[]{:S(2)}) copy-start(s32[256]{0:T(256)} %param.17) | copy-start | bytes 3076
  0.6 70.8 %copy-start.7 = (bf16[1,1,576,16]{2,3,1,0:T(8,128)(2,1)S(1)}, bf16[1,1,576,16]{2,3,1,0:T(8,128)(2,1)}, u32[]{:S(2)}) copy-start(bf16[1,1,576,16]{2,3,1,0:T(8,128)(2,1)} %param.15) | copy-start | bytes 55300
  0.7 70.8 %copy-start.8 = (bf16[1,1,576,16]{2,3,1,0:T(8,128)(2,1)S(1)}, bf16[1,1,576,16]{2,3,1,0:T(8,128)(2,1)}, u32[]{:S(2)}) copy-start(bf16[1,1,576,16]{2,3,1,0:T(8,128)(2,1)} %param.16) | copy-start | bytes 55300
  0.7 70.8 %copy-start.9 = (s32[1,576]{1,0:T(1,128)S(1)}, s32[1,576]{1,0:T(1,128)}, u32[]{:S(2)}) copy-start(s32[1,576]{1,0:T(1,128)} %row_ref.1) | copy-start | bytes 6916
  0.7 70.8 %copy-start.10 = (s32[1,576]{1,0:T(1,128)S(1)}, s32[1,576]{1,0:T(1,128)}, u32[]{:S(2)}) copy-start(s32[1,576]{1,0:T(1,128)} %expert_ref.1) | copy-start | bytes 6916
  0.7 70.8 %copy-start.11 = (s32[1,64]{1,0:T(1,128)S(1)}, s32[1,64]{1,0:T(1,128)}, u32[]{:S(2)}) copy-start(s32[1,64]{1,0:T(1,128)} %count_ref.1) | copy-start | bytes 772
  0.7 70.8 %copy-start.12 = (s32[1,64]{1,0:T(1,128)S(1)}, s32[1,64]{1,0:T(1,128)}, u32[]{:S(2)}) copy-start(s32[1,64]{1,0:T(1,128)} %offset_ref.1) | copy-start | bytes 772
